TPU v7x, 1024 devices: a whole 4x8x16 slice. The times are simulated.
1024 devices in a mesh: fourier: 64 (over y, x, core), elem: 16 (over z).
Axes of the slice: x: 4, y: 8, z: 16, core: 2. Of those that a mesh axis runs over, the one named last changes fastest.
Arguments:
- vel_az: float32 [256, 2048, 256], P('fourier', 'elem'), may hold values from -1.5 to 1.5
- vel_rad: float32 [256, 2048, 256], P('fourier', 'elem'), may hold values from -1.5 to 1.5
- axial: float32 [256, 2048, 256], P('fourier', 'elem'), may hold values from -6 to 6
- metric_az: float32 [256, 32], P('elem'), may hold values from 0.4 to 2.5
- metric_rad: float32 [256, 32], P('elem'), may hold values from 0.4 to 2.5
Outputs:
- velocity_modes: float32 [256, 2048, 256], P('fourier', 'elem')
All inputs are finite; a program needn't handle non-finite values.
Results may differ from a plain program's by a relative error of at most 0.0001.
Values sent between devices are 32-bit elements; how exact they have to be, the bound alone decides.
A program may use at most 32 MiB of HBM per device.

v0:
```python
import math

import jax
import jax.numpy as jnp
import numpy as np
from jax import lax
from jax.sharding import PartitionSpec as P

PLANES = 256
NODES = 8
ITERS = 2


INV_DT = 2.0
INV_NU = 2.0
SHIFT = 4.0
BETA_UNIT = 0.03125
HIGH = lax.Precision.HIGHEST


def padded_2(block, sides, width):
    for axis, dim in sides:
        count = lax.axis_size(axis)
        forward = [(i, i + 1) for i in range(count - 1)]
        forward.append((count - 1, 0))
        backward = [(target, source) for source, target in forward]
        low = lax.ppermute(
            lax.slice_in_dim(block, block.shape[dim] - width, None, axis=dim), axis, forward
        )
        high = lax.ppermute(lax.slice_in_dim(block, 0, width, axis=dim), axis, backward)
        block = jnp.concatenate([low, block, high], axis=dim)
    return block


def gll_tables():
    points = np.array(
        [
            -1.0,
            -0.8717401485096066,
            -0.5917001814331423,
            -0.2092992179024789,
            0.2092992179024789,
            0.5917001814331423,
            0.8717401485096066,
            1.0,
        ]
    )
    gll_weights = np.array(
        [
            0.03571428571428571,
            0.2107042271435061,
            0.3411226924835044,
            0.4124587946587038,
            0.4124587946587038,
            0.3411226924835044,
            0.2107042271435061,
            0.03571428571428571,
        ]
    )
    number = points.shape[0]
    scales = np.array(
        [
            np.prod([points[col_at] - points[other] for other in range(number) if other != col_at])
            for col_at in range(number)
        ]
    )
    derivative = np.zeros((number, number))
    for row_at in range(number):
        for col_at in range(number):
            if row_at != col_at:
                derivative[row_at, col_at] = scales[row_at] / (
                    scales[col_at] * (points[row_at] - points[col_at])
                )
    for row_at in range(number):
        derivative[row_at, row_at] = -np.sum(derivative[row_at])
    stiffness = derivative.T @ (gll_weights[:, None] * derivative)
    return (
        jnp.asarray(gll_weights, jnp.float32),
        jnp.asarray(derivative, jnp.float32),
        jnp.asarray(stiffness, jnp.float32),
    )


def mode_table(planes):
    mode_ids = jnp.arange(planes, dtype=jnp.int32)
    waves = jnp.where(mode_ids == 1, planes // 2, mode_ids // 2)
    plane_ids = jnp.arange(planes, dtype=jnp.int32)
    phase = waves[:, None] * plane_ids[None, :] % planes
    angles = phase.astype(jnp.float32) * (2.0 * math.pi / planes)
    odd_rows = (mode_ids % 2 == 1) & (mode_ids > 1)
    table = jnp.where(odd_rows[:, None], -jnp.sin(angles), jnp.cos(angles))
    return table / math.sqrt(planes)


def spread(values):
    return jnp.repeat(jnp.repeat(values, NODES, axis=0), NODES, axis=1)


def shards(vel_az, vel_rad, axial, metric_az, metric_rad):
    gll_weights, derivative, stiffness = gll_tables()
    rows_az = axial.shape[1]
    rows_rad = axial.shape[2]
    elems_az, elems_rad = metric_az.shape
    metric_a = spread(metric_az)
    metric_r = spread(metric_rad)
    weight_a = jnp.tile(gll_weights, elems_az)[:, None]
    weight_r = jnp.tile(gll_weights, elems_rad)[None, :]
    eye_az = jnp.eye(elems_az, dtype=jnp.float32)
    eye_rad = jnp.eye(elems_rad, dtype=jnp.float32)
    deriv_az = jnp.kron(eye_az, derivative)
    deriv_rad = jnp.kron(eye_rad, derivative)
    stiff_az = jnp.kron(eye_az, stiffness)
    stiff_rad = jnp.kron(eye_rad, stiffness)
    grad_az = jnp.einsum("ab,pbr->par", deriv_az, axial, precision=HIGH) * metric_a
    grad_rad = jnp.einsum("pas,rs->par", axial, deriv_rad, precision=HIGH) * metric_r
    nonlinear = vel_az * grad_az + vel_rad * grad_rad
    drive = (INV_DT * axial - nonlinear) * INV_NU
    table = mode_table(PLANES)
    coefficients = jnp.einsum(
        "mp,pak->mak",
        table,
        lax.all_to_all(drive, "fourier", split_axis=1, concat_axis=0, tiled=True),
        precision=HIGH,
    )
    spectral = lax.all_to_all(coefficients, "fourier", split_axis=0, concat_axis=1, tiled=True)
    local_modes = spectral.shape[0]
    mode_ids = lax.axis_index("fourier") * local_modes + jnp.arange(local_modes, dtype=jnp.int32)
    my_waves = jnp.where(mode_ids == 1, PLANES // 2, mode_ids // 2)
    shift_coef = (SHIFT + (my_waves.astype(jnp.float32) * BETA_UNIT) ** 2)[:, None, None]
    area = 1.0 / (metric_a * metric_r)
    mass_nodes = weight_a * weight_r * area
    coef_az = metric_a / metric_r * weight_r
    coef_rad = metric_r / metric_a * weight_a
    pos_az = jnp.arange(rows_az, dtype=jnp.int32)
    pos_rad = jnp.arange(rows_rad, dtype=jnp.int32)
    place_az = pos_az % NODES
    place_rad = pos_rad % NODES
    keep = jnp.where(pos_rad == rows_rad - 1, 0.0, 1.0).astype(jnp.float32)[None, :]
    edge_az = (place_az == 0) | (place_az == NODES - 1)
    shared_rad = (place_rad == NODES - 1) & (pos_rad < rows_rad - 1) | (place_rad == 0) & (
        pos_rad > 0
    )
    count_a = jnp.where(edge_az, 2.0, 1.0).astype(jnp.float32)[:, None]
    count_r = jnp.where(shared_rad, 2.0, 1.0).astype(jnp.float32)[None, :]
    inner_weight = 1.0 / (count_a * count_r)
    partner = jnp.where(
        (place_rad == NODES - 1) & (pos_rad < rows_rad - 1),
        pos_rad + 1,
        jnp.where((place_rad == 0) & (pos_rad > 0), pos_rad - 1, -1),
    )
    pairing = (pos_rad[:, None] == partner[None, :]).astype(jnp.float32)
    first_row = (place_az == 0)[None, :, None]
    last_row = (place_az == NODES - 1)[None, :, None]

    def assemble(field):
        joined = field + jnp.einsum("mas,sr->mar", field, pairing, precision=HIGH)
        padded = padded_2(joined, (("elem", 1),), 1)
        return (
            joined
            + jnp.where(last_row, padded[:, 2:], 0.0)
            + jnp.where(first_row, padded[:, :-2], 0.0)
        )

    def local_inner(left, right):
        return jnp.sum(inner_weight * left * right, axis=(1, 2))

    def widen(values):
        return values[:, None, None]

    right_side = assemble(mass_nodes * spectral) * keep
    solution = jnp.zeros_like(right_side)

    def squares(field):
        return lax.psum(local_inner(field, field), "elem")

    residual = right_side
    direction = right_side
    norm_now = squares(residual)
    for iteration in range(ITERS):
        along_az = jnp.einsum("ab,mbr->mar", stiff_az, direction, precision=HIGH) * coef_az
        along_rad = jnp.einsum("mas,rs->mar", direction, stiff_rad, precision=HIGH) * coef_rad
        image = assemble(along_az + along_rad + shift_coef * mass_nodes * direction) * keep
        alpha = norm_now / lax.psum(local_inner(direction, image), "elem")
        solution = solution + widen(alpha) * direction
        if iteration + 1 < ITERS:
            residual = residual - widen(alpha) * image
            norm_next = squares(residual)
            direction = residual + widen(norm_next / norm_now) * direction
            norm_now = norm_next
    return solution


def solution(mesh):
    in_specs = (
        P("fourier", "elem", None),
        P("fourier", "elem", None),
        P("fourier", "elem", None),
        P("elem", None),
        P("elem", None),
    )
    out_specs = P("fourier", "elem", None)
    return jax.shard_map(shards, mesh=mesh, in_specs=in_specs, out_specs=out_specs, check_vma=False)
```

profile of v0, /device:TPU:16, one launch (start us, length us, event | category | flops | bytes accessed | tf_op | source)
XLA Modules:
  0.0 212.7 jit_solution(3462128444096912627)
XLA Ops:
  0.0 0.7 copy-done
  0.8 0.7 broadcast_bitcast_fusion.3
  1.5 0.7 copy.35
  2.2 5.0 %broadcast_multiply_fusion.1 = (f32[32,8,32,8]{3,2,1,0:T(8,128)}, f32[32,8,32,8]{3,2,1,0:T(8,128)}) fusion(f32[8,8]{1,0:T(8,128)} %constant.119.clone, f32[32,32]{1,0:T(8,128)S(1)} %fusion.69, f32[8,8]{1,0:T(8,128)} %constant.120.clone), kind=kLoop, calls=%fused_computation.1 | loop fusion | flops 131072 | bytes 528896 | tf_op jit(solution)/shard_map/jit(kron)/mul | solution.py:111
  7.2 4.1 %reshape.294 = f32[256,256,1]{1,0,2:T(8,128)S(1)} reshape(f32[32,8,32,8]{3,2,1,0:T(8,128)} %get-tuple-element.18) | data formatting | bytes 524288 | tf_op jit(solution)/shard_map/jit(kron)/mul | solution.py:111
  11.3 0.8 copy.40
  12.1 0.9 broadcast_multiply_fusion.2
  13.0 1.1 reshape.293
  14.1 0.7 broadcast_bitcast_fusion.1
  14.9 1.5 fusion.12
  16.5 1.8 fusion.10
  18.3 1.1 copy.41
  19.4 17.2 %all-to-all-start = ((f32[4,128,256]{2,0,1:T(4,128)}), f32[4,128,256]{2,0,1:T(4,128)S(1)}, u32[]{:S(2)}, u32[]{:S(2)}) async-start(f32[4,128,256]{2,0,1:T(4,128)} %copy.41), calls=%async_computation | async-start | bytes 1048576 | tf_op jit(solution)/shard_map/all_to_all | solution.py:122
  36.6 17.9 %all-to-all-done = f32[4,128,256]{2,0,1:T(4,128)S(1)} async-done(((f32[4,128,256]{2,0,1:T(4,128)}), f32[4,128,256]{2,0,1:T(4,128)S(1)}, u32[]{:S(2)}, u32[]{:S(2)}) %all-to-all-start) | async-done | bytes 524320 | tf_op jit(solution)/shard_map/all_to_all | solution.py:122
  54.6 0.2 all_to_all.29
  54.8 1.7 fusion.37
  56.5 1.2 copy.43
  57.7 5.5 %all-to-all-start.1 = ((f32[256,2,256]{2,1,0:T(2,128)}), f32[256,2,256]{2,1,0:T(2,128)S(1)}, u32[]{:S(2)}, u32[]{:S(2)}) async-start(f32[256,2,256]{2,1,0:T(2,128)} %copy.43), calls=%async_computation.1 | async-start | bytes 1048576 | tf_op jit(solution)/shard_map/all_to_all | solution.py:125
  63.4 0.1 fusion.55
  63.7 17.3 %all-to-all-done.1 = f32[256,2,256]{2,1,0:T(2,128)S(1)} async-done(((f32[256,2,256]{2,1,0:T(2,128)}), f32[256,2,256]{2,1,0:T(2,128)S(1)}, u32[]{:S(2)}, u32[]{:S(2)}) %all-to-all-start.1) | async-done | bytes 524320 | tf_op jit(solution)/shard_map/all_to_all | solution.py:125
  81.0 0.2 copy.50
  81.2 0.4 all_to_all.33
  81.6 0.4 convolution_add_fusion.2
  82.0 1.9 collective-permute-start.1
  84.0 11.7 %collective-permute-start = (f32[4,1,256]{2,1,0:T(1,128)S(1)}, f32[4,1,256]{2,1,0:T(1,128)S(1)}, u32[]{:S(2)}, u32[]{:S(2)}) collective-permute-start(f32[4,1,256]{2,1,0:T(1,128)S(1)} %get-tuple-element.13), channel_id=1, source_target_pairs={{1,0},{2,1},{3,2},{4,3},{5,4},{6,5},{7,6},{8,7},{9,8},{10,9},{11,1... | collective-permute-start | bytes 12296 | tf_op jit(solution)/shard_map/ppermute | solution.py:30
  95.7 4.0 %reshape.298 = f32[256,256,1]{1,0,2:T(8,128)S(1)} reshape(f32[32,8,32,8]{3,2,1,0:T(8,128)} %get-tuple-element.19) | data formatting | bytes 524288 | tf_op jit(solution)/shard_map/jit(kron)/mul | solution.py:113
  99.8 0.5 reshape.297
  100.4 0.7 convolution_multiply_fusion.2
  101.2 1.0 fusion.2
  102.2 0.4 convolution_add_fusion.1
  102.7 1.9 collective-permute-start.3
  104.6 5.1 %collective-permute-start.2 = (f32[4,1,256]{2,1,0:T(1,128)S(1)}, f32[4,1,256]{2,1,0:T(1,128)S(1)}, u32[]{:S(2)}, u32[]{:S(2)}) collective-permute-start(f32[4,1,256]{2,1,0:T(1,128)S(1)} %get-tuple-element.11), channel_id=1, source_target_pairs={{1,0},{2,1},{3,2},{4,3},{5,4},{6,5},{7,6},{8,7},{9,8},{10,9},{11,1... | collective-permute-start | bytes 12296 | tf_op jit(solution)/shard_map/ppermute | solution.py:30
  109.7 0.1 multiply_divide_fusion
  109.9 1.1 collective-permute-done.2
  111.0 0.7 fusion.14
  111.7 30.5 %all-reduce = (f32[4]{0:T(128)S(1)}, f32[4]{0:T(128)S(1)}) all-reduce(f32[4]{0:T(128)S(1)} %get-tuple-element.6, f32[4]{0:T(128)S(1)} %get-tuple-element.5), channel_id=1, replica_groups=mesh['fourier'=64,'elem'=16] {'elem'}, use_global_device_ids=true, to_apply=%region_1.2 | all-reduce | flops 8 | bytes 64 | tf_op jit(solution)/shard_map/psum | solution.py:174
  142.2 0.6 fusion.15
  142.8 27.0 %psum.30 = f32[4]{0:T(128)S(1)} all-reduce(f32[4]{0:T(128)S(1)} %fusion.15), channel_id=1, replica_groups=mesh['fourier'=64,'elem'=16] {'elem'}, use_global_device_ids=true, to_apply=%region_5.6 | all-reduce | flops 4 | bytes 32 | tf_op jit(solution)/shard_map/psum | solution.py:174
  169.8 0.7 multiply_add_fusion.1
  170.5 0.6 convolution_multiply_fusion.1
  171.1 0.7 fusion.5
  171.8 0.4 convolution_add_fusion
  172.3 3.9 %collective-permute-start.5 = (f32[4,1,256]{2,1,0:T(1,128)S(1)}, f32[4,1,256]{2,1,0:T(1,128)S(1)}, u32[]{:S(2)}, u32[]{:S(2)}) collective-permute-start(f32[4,1,256]{2,1,0:T(1,128)S(1)} %get-tuple-element.10), channel_id=1, source_target_pairs={{0,1},{1,2},{2,3},{3,4},{4,5},{5,6},{6,7},{7,8},{8,9},{9,10},{10,1... | collective-permute-start | bytes 12296 | tf_op jit(solution)/shard_map/ppermute | solution.py:27
  176.2 3.1 %collective-permute-start.4 = (f32[4,1,256]{2,1,0:T(1,128)S(1)}, f32[4,1,256]{2,1,0:T(1,128)S(1)}, u32[]{:S(2)}, u32[]{:S(2)}) collective-permute-start(f32[4,1,256]{2,1,0:T(1,128)S(1)} %get-tuple-element.9), channel_id=1, source_target_pairs={{1,0},{2,1},{3,2},{4,3},{5,4},{6,5},{7,6},{8,7},{9,8},{10,9},{11,1... | collective-permute-start | bytes 12296 | tf_op jit(solution)/shard_map/ppermute | solution.py:30
  179.3 2.3 %collective-permute-done.4 = f32[4,1,256]{2,1,0:T(1,128)S(1)} collective-permute-done((f32[4,1,256]{2,1,0:T(1,128)S(1)}, f32[4,1,256]{2,1,0:T(1,128)S(1)}, u32[]{:S(2)}, u32[]{:S(2)}) %collective-permute-start.4) | collective-permute-done | bytes 4128 | tf_op jit(solution)/shard_map/ppermute | solution.py:30
  181.7 0.4 fusion.20
  182.1 29.4 %psum.31 = f32[4]{0:T(128)S(1)} all-reduce(f32[4]{0:T(128)S(1)} %fusion.20), channel_id=1, replica_groups=mesh['fourier'=64,'elem'=16] {'elem'}, use_global_device_ids=true, to_apply=%region_7.8 | all-reduce | flops 4 | bytes 32 | tf_op jit(solution)/shard_map/psum | solution.py:183
  211.5 1.1 multiply_add_fusion
  (46 shorter events, 0.9 us)
Async XLA Ops:
  0.0 0.7 copy-start
  0.8 10.6 %copy-start.3 = (f32[128,32]{0,1:T(8,128)}, f32[128,32]{0,1:T(8,128)S(1)}, u32[]{:S(2)}) copy-start(f32[128,32]{0,1:T(8,128)S(1)} %copy.36) | copy-start | bytes 49156
  7.2 7.7 %copy-start.1 = (f32[4,128,256]{2,1,0:T(8,128)S(1)}, f32[4,128,256]{2,1,0:T(8,128)}, u32[]{:S(2)}) copy-start(f32[4,128,256]{2,1,0:T(8,128)} %param.10) | copy-start | bytes 1572868
  7.2 7.7 %copy-start.2 = (f32[4,128,256]{2,1,0:T(8,128)S(1)}, f32[4,128,256]{2,1,0:T(8,128)}, u32[]{:S(2)}) copy-start(f32[4,128,256]{2,1,0:T(8,128)} %param.9) | copy-start | bytes 1572868
  18.3 45.0 %copy-start.6 = (f32[8]{0:T(128)S(1)}, f32[8]{0:T(128)}, u32[]{:S(2)}) copy-start(f32[8]{0:T(128)} %constant.118.clone) | copy-start | bytes 100
  18.3 45.2 %copy-start.4 = (f32[128,32]{0,1:T(8,128)S(1)}, f32[128,32]{0,1:T(8,128)}, u32[]{:S(2)}) copy-start(f32[128,32]{0,1:T(8,128)} %copy-done.3) | copy-start | bytes 49156
  18.3 45.2 %copy-start.5 = (f32[128,32]{0,1:T(8,128)S(1)}, f32[128,32]{0,1:T(8,128)}, u32[]{:S(2)}) copy-start(f32[128,32]{0,1:T(8,128)} %copy.35) | copy-start | bytes 49156
  19.4 35.1 %all-to-all-start = ((f32[4,128,256]{2,0,1:T(4,128)}), f32[4,128,256]{2,0,1:T(4,128)S(1)}, u32[]{:S(2)}, u32[]{:S(2)}) async-start(f32[4,128,256]{2,0,1:T(4,128)} %copy.41), calls=%async_computation | async-start | bytes 1048576 | tf_op jit(solution)/shard_map/all_to_all | solution.py:122
  57.7 23.3 %all-to-all-start.1 = ((f32[256,2,256]{2,1,0:T(2,128)}), f32[256,2,256]{2,1,0:T(2,128)S(1)}, u32[]{:S(2)}, u32[]{:S(2)}) async-start(f32[256,2,256]{2,1,0:T(2,128)} %copy.43), calls=%async_computation.1 | async-start | bytes 1048576 | tf_op jit(solution)/shard_map/all_to_all | solution.py:125
  82.0 18.4 %collective-permute-start.1 = (f32[4,1,256]{2,1,0:T(1,128)S(1)}, f32[4,1,256]{2,1,0:T(1,128)S(1)}, u32[]{:S(2)}, u32[]{:S(2)}) collective-permute-start(f32[4,1,256]{2,1,0:T(1,128)S(1)} %get-tuple-element.14), channel_id=1, source_target_pairs={{0,1},{1,2},{2,3},{3,4},{4,5},{5,6},{6,7},{7,8},{8,9},{9,10},{10,1... | collective-permute-start | bytes 12296 | tf_op jit(solution)/shard_map/ppermute | solution.py:27
  84.0 16.5 %collective-permute-start = (f32[4,1,256]{2,1,0:T(1,128)S(1)}, f32[4,1,256]{2,1,0:T(1,128)S(1)}, u32[]{:S(2)}, u32[]{:S(2)}) collective-permute-start(f32[4,1,256]{2,1,0:T(1,128)S(1)} %get-tuple-element.13), channel_id=1, source_target_pairs={{1,0},{2,1},{3,2},{4,3},{5,4},{6,5},{7,6},{8,7},{9,8},{10,9},{11,1... | collective-permute-start | bytes 12296 | tf_op jit(solution)/shard_map/ppermute | solution.py:30
  102.7 7.3 %collective-permute-start.3 = (f32[4,1,256]{2,1,0:T(1,128)S(1)}, f32[4,1,256]{2,1,0:T(1,128)S(1)}, u32[]{:S(2)}, u32[]{:S(2)}) collective-permute-start(f32[4,1,256]{2,1,0:T(1,128)S(1)} %get-tuple-element.12), channel_id=1, source_target_pairs={{0,1},{1,2},{2,3},{3,4},{4,5},{5,6},{6,7},{7,8},{8,9},{9,10},{10,1... | collective-permute-start | bytes 12296 | tf_op jit(solution)/shard_map/ppermute | solution.py:27
  104.6 6.4 %collective-permute-start.2 = (f32[4,1,256]{2,1,0:T(1,128)S(1)}, f32[4,1,256]{2,1,0:T(1,128)S(1)}, u32[]{:S(2)}, u32[]{:S(2)}) collective-permute-start(f32[4,1,256]{2,1,0:T(1,128)S(1)} %get-tuple-element.11), channel_id=1, source_target_pairs={{1,0},{2,1},{3,2},{4,3},{5,4},{6,5},{7,6},{8,7},{9,8},{10,9},{11,1... | collective-permute-start | bytes 12296 | tf_op jit(solution)/shard_map/ppermute | solution.py:30
  172.3 7.1 %collective-permute-start.5 = (f32[4,1,256]{2,1,0:T(1,128)S(1)}, f32[4,1,256]{2,1,0:T(1,128)S(1)}, u32[]{:S(2)}, u32[]{:S(2)}) collective-permute-start(f32[4,1,256]{2,1,0:T(1,128)S(1)} %get-tuple-element.10), channel_id=1, source_target_pairs={{0,1},{1,2},{2,3},{3,4},{4,5},{5,6},{6,7},{7,8},{8,9},{9,10},{10,1... | collective-permute-start | bytes 12296 | tf_op jit(solution)/shard_map/ppermute | solution.py:27
  176.2 5.5 %collective-permute-start.4 = (f32[4,1,256]{2,1,0:T(1,128)S(1)}, f32[4,1,256]{2,1,0:T(1,128)S(1)}, u32[]{:S(2)}, u32[]{:S(2)}) collective-permute-start(f32[4,1,256]{2,1,0:T(1,128)S(1)} %get-tuple-element.9), channel_id=1, source_target_pairs={{1,0},{2,1},{3,2},{4,3},{5,4},{6,5},{7,6},{8,7},{9,8},{10,9},{11,1... | collective-permute-start | bytes 12296 | tf_op jit(solution)/shard_map/ppermute | solution.py:30
where the time goes:
time: 213 us
  blocking collectives  86.9 us (41%)
  starting transfers between devices  50.4 us (24%)
  waiting for transfers between devices  38.7 us (18%)
  local copies, waits for them, and re-layouts  17.1 us (8%)
  other arithmetic  9.73 us (5%)
  matrix products  9.34 us (4%)
    psum x2, blocking collectives, squares(): return lax.psum(local_inner(field, field), 'elem')  57.5 us
    psum x1, blocking collectives, shards(): alpha = norm_now / lax.psum(local_inner(direction, image), 'elem')  29.4 us
    ppermute x3, starting transfers between devices, padded_2(): lax.ppermute(lax.slice_in_dim(block, 0, width, axis=dim), axis, backward)  20 us
    all_to_all x1, waiting for transfers between devices, shards(): lax.all_to_all(drive, 'fourier', split_axis=1, concat_axis=0, tiled=True)  17.9 us
    all_to_all x1, waiting for transfers between devices, shards(): lax.all_to_all(coefficients, 'fourier', split_axis=0, concat_axis=1, tile...  17.3 us
    all_to_all x1, starting transfers between devices, shards(): lax.all_to_all(drive, 'fourier', split_axis=1, concat_axis=0, tiled=True)  17.2 us
    ppermute x3, starting transfers between devices, padded_2(): lax.ppermute(lax.slice_in_dim(block, block.shape[dim] - width, None, axis...  7.76 us
    all_to_all x1, starting transfers between devices, shards(): lax.all_to_all(coefficients, 'fourier', split_axis=0, concat_axis=1, tile...  5.51 us
  transfers between devices with their start and end apart: 8, of which 4 were waited for; matrix products, arithmetic and copies ran while one was open for 3% of the time, Pallas kernels for 0%

commit v1 on v0

v1 whole, which is shorter than its diff:
```python
import math

import jax
import jax.numpy as jnp
import ml_dtypes
import numpy as np
from jax import lax
from jax.experimental import pallas as pl
from jax.experimental.pallas import tpu as pltpu
from jax.sharding import PartitionSpec as P

MESH = pl.DeviceIdType.MESH
F32 = jnp.float32
BF16 = jnp.bfloat16
HIGH = lax.Precision.HIGHEST

PLANES = 256
NODES = 8
NF = 64
NZ = 16
ROWS = 128
COLS = 256
EZ = 16
UNIQUE = 7 * EZ
A_UNITS = 56
X_UNIT = 56
B_BASE = 57
UNITS = 99
PADDED = 105
FIRST = 64
EXTRA = (1, 27, 45)
SEAM = (0, 56, 57, 58, 59)

DR_H, DR_L, KR_H, KR_L, SR, ER, C_H, C_L = range(8)
DA_H, DA_L, KA_H, KA_L, RA_A, RA_B, EA_A, EA_B = range(8)


def gll_tables():
    points = np.array(
        [
            -1.0,
            -0.8717401485096066,
            -0.5917001814331423,
            -0.2092992179024789,
            0.2092992179024789,
            0.5917001814331423,
            0.8717401485096066,
            1.0,
        ]
    )
    gll_weights = np.array(
        [
            0.03571428571428571,
            0.2107042271435061,
            0.3411226924835044,
            0.4124587946587038,
            0.4124587946587038,
            0.3411226924835044,
            0.2107042271435061,
            0.03571428571428571,
        ]
    )
    number = points.shape[0]
    scales = np.array(
        [
            np.prod([points[col_at] - points[other] for other in range(number) if other != col_at])
            for col_at in range(number)
        ]
    )
    derivative = np.zeros((number, number))
    for row_at in range(number):
        for col_at in range(number):
            if row_at != col_at:
                derivative[row_at, col_at] = scales[row_at] / (
                    scales[col_at] * (points[row_at] - points[col_at])
                )
    for row_at in range(number):
        derivative[row_at, row_at] = -np.sum(derivative[row_at])
    stiffness = derivative.T @ (gll_weights[:, None] * derivative)
    return (
        gll_weights.astype(np.float32),
        derivative.astype(np.float32),
        stiffness.astype(np.float32),
    )


def mode_table():
    modes = np.arange(PLANES)
    waves = np.where(modes == 1, PLANES // 2, modes // 2)
    phase = waves[:, None] * np.arange(PLANES)[None, :] % PLANES
    angles = phase * (2.0 * math.pi / PLANES)
    odd = (modes % 2 == 1) & (modes > 1)
    return (np.where(odd[:, None], -np.sin(angles), np.cos(angles)) / math.sqrt(PLANES)).astype(
        np.float32
    )


def halves(matrix):
    high = matrix.astype(ml_dtypes.bfloat16)
    low = (matrix - high.astype(np.float32)).astype(ml_dtypes.bfloat16)
    return [high, low]


def row_maps():
    every = [(e, j) for e in range(EZ) for j in range(7)]
    first = {}
    for j in range(7):
        first[j] = (0, j)
        first[A_UNITS + j] = (EZ - 1, j)
    first[7] = (1, 0)
    left = [r for r in every if r not in first.values()]
    for at in range(2 * A_UNITS):
        if at not in first:
            first[at] = left.pop(0)
    second = {}
    for g in range(2):
        for q in range(4):
            j = g * 4 + q
            second[q * 16 + g] = (0, j) if j < 7 else (1, 0)
            if j < 7:
                second[(4 + q) * 16 + g] = (EZ - 1, j)
    left = [r for r in every if r not in second.values()]
    for block in range(8):
        for g in range(14):
            if block * 16 + g not in second:
                second[block * 16 + g] = left.pop(0)
    return first, second


def tables():
    weights, derivative, stiffness = gll_tables()
    w256, w128 = [], []
    w256 += halves(np.kron(np.eye(32, dtype=np.float32), derivative).T)
    w256 += halves(np.kron(np.eye(32, dtype=np.float32), stiffness).T)
    fold = np.zeros((COLS, COLS), np.float32)
    for s in range(COLS):
        c = 7 * (s // 8) + s % 8
        if c < 224:
            fold[s, c] = 1.0
    w256 += [fold.astype(ml_dtypes.bfloat16), fold.T.astype(ml_dtypes.bfloat16)]
    w256 += halves(mode_table())
    w128 += halves(np.kron(np.eye(EZ, dtype=np.float32), derivative))
    w128 += halves(np.kron(np.eye(EZ, dtype=np.float32), stiffness))
    first, second = row_maps()
    ra_a, ra_b, ea_a, ea_b = (np.zeros((ROWS, ROWS), np.float32) for _ in range(4))
    for packed, fold_rows, unfold_rows in ((first, ra_a, ea_a), (second, ra_b, ea_b)):
        for at, (e, j) in packed.items():
            fold_rows[at, 8 * e + j] = 1.0
            if j == 0 and e > 0:
                fold_rows[at, 8 * e - 1] = 1.0
            unfold_rows[:, at] = fold_rows[at]
    ea_a[ROWS - 1, UNIQUE] = 1.0
    ea_b[ROWS - 1, 14] = 1.0
    w128 += [m.astype(ml_dtypes.bfloat16) for m in (ra_a, ra_b, ea_a, ea_b)]
    weight_a = np.tile(weights, EZ)[:, None] * np.ones((1, COLS), np.float32)
    weight_r = np.tile(weights, 32)[None, :] * np.ones((ROWS, 1), np.float32)
    a, r = np.arange(ROWS), np.arange(COLS)
    count_a = np.where((a % 8 == 0) | (a % 8 == 7), 2.0, 1.0)
    count_r = np.where(((r % 8 == 7) & (r < 255)) | ((r % 8 == 0) & (r > 0)), 2.0, 1.0)
    inner = 1.0 / (count_a[:, None] * count_r[None, :])
    nodes = np.stack([weight_a, weight_r, inner]).astype(np.float32)
    return np.stack(w256), np.stack(w128), nodes, stiffness


def split(x):
    high = x.astype(BF16)
    return high, (x - high.astype(F32)).astype(BF16)


def dot(a, b):
    return jnp.dot(a, b, preferred_element_type=F32)


def left3(high, low, x):
    xh, xl = split(x)
    return dot(high, xh) + dot(high, xl) + dot(low, xh)


def right3(x, high, low):
    xh, xl = split(x)
    return dot(xh, high) + dot(xl, high) + dot(xh, low)


def left2(matrix, x):
    xh, xl = split(x)
    return dot(matrix, xh) + dot(matrix, xl)


def right2(x, matrix):
    xh, xl = split(x)
    return dot(xh, matrix) + dot(xl, matrix)


def roll(x, shift, axis):
    size = x.shape[axis]
    shift %= size
    return pltpu.roll(x, shift, axis) if shift else x


def lanes(shape):
    return lax.broadcasted_iota(jnp.int32, shape, 1)


def sublanes(shape):
    return lax.broadcasted_iota(jnp.int32, shape, 0)


def join_cols(field):
    lane = lanes(field.shape)
    total = (
        field
        + jnp.where((lane % 8 == 7), roll(field, -1, 1), 0.0)
        + jnp.where((lane % 8 == 0) & (lane > 0), roll(field, 1, 1), 0.0)
    )
    return jnp.where(lane == COLS - 1, 0.0, total)


def join_rows(field):
    row = sublanes(field.shape)
    return (
        field
        + jnp.where((row % 8 == 7) & (row < ROWS - 1), roll(field, -1, 0), 0.0)
        + jnp.where((row % 8 == 0) & (row > 0), roll(field, 1, 0), 0.0)
    )


def make_kernel(stiffness):
    def kernel(
        va_hbm,
        vr_hbm,
        ax_hbm,
        ma_hbm,
        mr_hbm,
        w256_hbm,
        w128_hbm,
        nodes_hbm,
        out_ref,
        va,
        vr,
        ax,
        ma_s,
        mr_s,
        w256,
        w128,
        nodes,
        metric,
        mass,
        coef,
        packed_a,
        packed_b,
        send1,
        recv1,
        send2,
        recv2,
        seam_s,
        seam_r,
        edge_s,
        edge_r,
        b_s,
        v_s,
        mrow,
        mom_s,
        mom_r,
        in_sem,
        s1,
        r1,
        s2,
        r2,
        hs,
        hr,
        ms,
        mr_sem,
    ):
        me = lax.axis_index("fourier")
        z = lax.axis_index("elem")
        up, down = lax.rem(z + 1, NZ), lax.rem(z + NZ - 1, NZ)

        loads = [
            pltpu.make_async_copy(src, dst, in_sem.at[i])
            for i, (src, dst) in enumerate(
                (
                    (ma_hbm, ma_s),
                    (mr_hbm, mr_s),
                    (nodes_hbm, nodes),
                    (w128_hbm, w128),
                    (ax_hbm, ax),
                    (w256_hbm, w256),
                    (va_hbm, va),
                    (vr_hbm, vr),
                )
            )
        ]
        for load in loads:
            load.start()

        barrier = pltpu.get_barrier_semaphore()

        def greet_f(k, carry):
            pl.semaphore_signal(
                barrier, inc=1, device_id=(lax.rem(me + k, NF), z), device_id_type=MESH
            )
            return carry

        def greet_z(k, carry):
            pl.semaphore_signal(
                barrier, inc=1, device_id=(me, lax.rem(z + k, NZ)), device_id_type=MESH
            )
            return carry

        recv2[pl.ds(UNITS * 8, (PADDED - UNITS) * 8), :] = jnp.zeros(
            ((PADDED - UNITS) * 8, 128), F32
        )
        lax.fori_loop(1, NZ, greet_z, 0)
        lax.fori_loop(1, NF, greet_f, 0)

        for load in loads[:3]:
            load.wait()
        up_rows = (lanes((ROWS, EZ)) == sublanes((ROWS, EZ)) // 8).astype(F32)
        up_cols = (sublanes((32, COLS)) == lanes((32, COLS)) // 8).astype(F32)

        def widen(values):
            tall = jnp.dot(up_rows, values, precision=HIGH, preferred_element_type=F32)
            return jnp.dot(tall, up_cols, precision=HIGH, preferred_element_type=F32)

        metric_a = widen(ma_s[...])
        metric_r = widen(mr_s[...])
        weight_a, weight_r = nodes[0], nodes[1]
        metric[0] = metric_a
        metric[1] = metric_r
        mass[...] = weight_a * weight_r / (metric_a * metric_r)
        coef[0] = metric_a / metric_r * weight_r
        coef[1] = metric_r / metric_a * weight_a

        for load in loads[3:]:
            load.wait()

        def drive_plane(p, carry):
            x = ax[p]
            xh, xl = split(x)
            grad_a = dot(w128[DA_H], xh) + dot(w128[DA_H], xl) + dot(w128[DA_L], xh)
            grad_r = dot(xh, w256[DR_H]) + dot(xl, w256[DR_H]) + dot(xh, w256[DR_L])
            nonlinear = va[p] * (grad_a * metric[0]) + vr[p] * (grad_r * metric[1])
            loaded = (2.0 * x - nonlinear) * 2.0 * mass[...]
            folded = right2(loaded, w256[SR])
            b_s[p] = folded
            high, low = split(folded)
            packed_a[p] = dot(w128[RA_A], high[:, :128]) + dot(w128[RA_A], low[:, :128])
            packed_b[p] = dot(w128[RA_B], high[:, 128:]) + dot(w128[RA_B], low[:, 128:])
            return carry

        lax.fori_loop(0, 4, drive_plane, 0)

        lane128 = lanes((16, 128))
        for p in range(4):
            seam_s[2 * p : 2 * p + 1, :] = b_s[p, 0:1, :]
            seam_s[2 * p + 1 : 2 * p + 2, :] = b_s[p, ROWS - 1 : ROWS, :]
            for h in range(2):
                send1[pl.ds(2 * p + h, A_UNITS, stride=8), :] = packed_a[
                    p, h * A_UNITS : (h + 1) * A_UNITS, :
                ]
                quarters = [
                    packed_b[p, (4 * h + q) * 16 : (4 * h + q + 1) * 16, :] for q in range(4)
                ]
                for t in range(3):
                    tile = roll(quarters[0], -32 * t, 1)
                    for q in range(1, 4):
                        tile = jnp.where(lane128 >= 32 * q, roll(quarters[q], 32 * (q - t), 1), tile)
                    send1[pl.ds((B_BASE + t) * 8 + 2 * p + h, 16, stride=24), :] = tile

        pl.semaphore_wait(barrier, NF - 1 + NZ - 1)

        def exchange(src, dst, at):
            copies = [
                pltpu.make_async_remote_copy(
                    src_ref=src,
                    dst_ref=dst.at[side],
                    send_sem=hs.at[at + side],
                    recv_sem=hr.at[at + side],
                    device_id=(me, target),
                    device_id_type=MESH,
                )
                for side, target in ((0, up), (1, down))
            ]
            for copy in copies:
                copy.start()
            return copies

        seam = exchange(seam_s, seam_r, 0)

        def tile_at(index):
            return pl.ds(pl.multiple_of(index * 8, 8), 8)

        def send_plane(unit, slot, target):
            pltpu.make_async_remote_copy(
                src_ref=send1.at[tile_at(unit), :],
                dst_ref=recv1.at[slot, tile_at(me), :],
                send_sem=s1.at[slot],
                recv_sem=r1.at[slot],
                device_id=(target, z),
                device_id_type=MESH,
            ).start()

        def first_chunk(k, carry):
            target = lax.rem(me + k, NF)
            waits = target == 0
            for unit in SEAM[1:]:
                waits = waits | (target == unit)

            @pl.when(jnp.logical_not(waits))
            def _():
                send_plane(target, 0, target)

            return carry

        lax.fori_loop(1, NF, first_chunk, 0)

        for copy in seam:
            copy.wait()
        own = seam_s[...]
        below, above = seam_r[0], seam_r[1]
        even = sublanes((8, 128)) % 2 == 0
        add_a = roll(below[:, :128], -1, 0)
        add_b = roll(below[:, 128:], -1, 0)
        lane = lanes((8, 128))
        send1[0:8, :] = send1[0:8, :] + jnp.where(even, add_a, 0.0)
        for t in range(3):
            at = (B_BASE + t) * 8
            send1[at : at + 8, :] = send1[at : at + 8, :] + jnp.where(
                even & (lane < 32), roll(add_b, -32 * t, 1), 0.0
            )
        top_a = roll(own[:, :128], -1, 0) + above[:, :128]
        top_b = own[:, 128:] + roll(above[:, 128:], 1, 0)
        send1[X_UNIT * 8 : X_UNIT * 8 + 8, :] = jnp.where(even, top_a, top_b)

        for unit in SEAM:

            @pl.when(me != unit)
            def _(unit=unit):
                send_plane(unit, 0, unit)

        def second_chunk(k, carry):
            chip = lax.rem(me // 2 + k, NF // 2)

            @pl.when(2 * chip != me)
            def _():
                send_plane(FIRST + chip, 1, 2 * chip)

            return carry

        lax.fori_loop(0, NF // 2, second_chunk, 0)
        for at, target in enumerate(EXTRA):

            @pl.when(me != target)
            def _(at=at, target=target):
                send_plane(FIRST + NF // 2 + at, 1, target)

        unit1 = FIRST + me // 2
        owner1 = me % 2 == 0
        for at, target in enumerate(EXTRA):
            unit1 = jnp.where(me == target, FIRST + NF // 2 + at, unit1)
            owner1 = owner1 | (me == target)

        recv1[0, tile_at(me), :] = send1[tile_at(me), :]

        def await_tiles(ref, count, sem):
            view = ref.at[pl.ds(0, count * 8), :]
            pltpu.make_async_copy(view, view, sem).wait()

        def transform(slot, unit):
            x = jnp.concatenate(
                [recv1[slot, pl.ds(h, PLANES, stride=2), :] for h in range(2)], axis=1
            )
            y = left3(w256[C_H], w256[C_L], x)
            for h in range(2):
                send2[slot, pl.ds(h, PLANES, stride=2), :] = y[:, 128 * h : 128 * (h + 1)]

            def send_modes(k, carry):
                target = lax.rem(me + k, NF)
                pltpu.make_async_remote_copy(
                    src_ref=send2.at[slot, tile_at(target), :],
                    dst_ref=recv2.at[tile_at(unit), :],
                    send_sem=s2.at[slot],
                    recv_sem=r2.at[slot],
                    device_id=(target, z),
                    device_id_type=MESH,
                ).start()
                return carry

            lax.fori_loop(1, NF, send_modes, 0)
            recv2[tile_at(unit), :] = send2[slot, tile_at(me), :]

        await_tiles(recv1.at[0], NF - 1, r1.at[0])
        transform(0, me)

        @pl.when(owner1)
        def _():
            recv1[1, tile_at(me), :] = send1[tile_at(unit1), :]
            await_tiles(recv1.at[1], NF - 1, r1.at[1])
            transform(1, unit1)

        await_tiles(recv2, NF - 1, r2.at[0])
        sub = sublanes((8, COLS))
        low_side = sub % 2 == 0
        x_tile = recv2[X_UNIT * 8 : X_UNIT * 8 + 8, :]
        edge_rows = []
        for j in range(8):
            g, q = j // 4, j % 4
            part_a = recv2[8 * j : 8 * j + 8, :]
            pieces = [
                recv2[(B_BASE + 3 * g + t) * 8 : (B_BASE + 3 * g + t) * 8 + 8, :] for t in range(3)
            ]
            part_b = roll(pieces[0], -32 * q, 1)
            for t in range(1, 3):
                part_b = jnp.where(lane >= 32 * t, roll(pieces[t], 32 * (t - q), 1), part_b)
            if j == 7:
                part_a = jnp.where(even, part_a, roll(x_tile, 1, 0))
                part_b = jnp.where(even, part_b, x_tile)
            edge_rows.append(jnp.concatenate([part_a, part_b], axis=1))
        edge = right2(jnp.concatenate(edge_rows, axis=0), w256[ER])
        along_a = jnp.zeros((8, COLS), F32)
        for j in range(8):
            factor = jnp.where(low_side, float(stiffness[0, j]), float(stiffness[7, j]))
            along_a = along_a + factor * edge[8 * j : 8 * j + 8]
        chosen = jnp.where(low_side, edge[0:8], edge[56:64])
        along_r = right3(chosen, w256[KR_H], w256[KR_L])

        def edge_coef(ref):
            return jnp.where(low_side, ref[0:1, :], ref[ROWS - 1 : ROWS, :])

        def shift_of(mode):
            wave = jnp.where(mode == 1, PLANES // 2, mode // 2)
            return 4.0 + (wave.astype(F32) * 0.03125) * (wave.astype(F32) * 0.03125)

        edge_shift = shift_of(4 * me + sub // 2)
        image = (
            edge_coef(coef.at[0]) * along_a
            + edge_coef(coef.at[1]) * along_r
            + edge_shift * edge_coef(mass) * chosen
        )
        edge_s[...] = join_cols(image)
        edges = exchange(edge_s, edge_r, 2)

        for p in range(4):
            for h in range(2):
                packed_a[p, h * A_UNITS : (h + 1) * A_UNITS, :] = recv2[
                    pl.ds(2 * p + h, A_UNITS, stride=8), :
                ]
            packed_a[p, UNIQUE : UNIQUE + 8, :] = jnp.where(
                sublanes((8, 128)) == 0, x_tile[2 * p : 2 * p + 1, :], 0.0
            )
            packed_a[p, UNIQUE + 8 : ROWS, :] = jnp.zeros((8, 128), F32)

        for copy in edges:
            copy.wait()

        @pl.when(owner1)
        def _():
            await_tiles(recv2, UNITS - FIRST - 1, r2.at[1])

        @pl.when(jnp.logical_not(owner1))
        def _():
            await_tiles(recv2, UNITS - FIRST, r2.at[1])

        for p in range(4):
            for h in range(2):
                pieces = [
                    recv2[pl.ds((B_BASE + t) * 8 + 2 * p + h, 16, stride=24), :] for t in range(3)
                ]
                for q in range(4):
                    part_b = roll(pieces[0], -32 * q, 1)
                    for t in range(1, 3):
                        part_b = jnp.where(
                            lane128 >= 32 * t, roll(pieces[t], 32 * (t - q), 1), part_b
                        )
                    if h == 0 and q == 0:
                        part_b = jnp.where(
                            sublanes((16, 128)) == 14, x_tile[2 * p + 1 : 2 * p + 2, :], part_b
                        )
                    packed_b[p, (4 * h + q) * 16 : (4 * h + q + 1) * 16, :] = part_b

        def operate(field, shift):
            high, low = split(field)
            along_a = dot(w128[KA_H], high) + dot(w128[KA_H], low) + dot(w128[KA_L], high)
            along_r = dot(high, w256[KR_H]) + dot(low, w256[KR_H]) + dot(high, w256[KR_L])
            return along_a * coef[0] + along_r * coef[1] + shift * mass[...] * field

        def total(field):
            row = jnp.sum(field, axis=0, keepdims=True)
            return row[:, :128] + row[:, 128:]

        row_ids = sublanes((ROWS, COLS))

        def mode_step(p, carry):
            wide = jnp.concatenate(
                [left2(w128[EA_A], packed_a[p]), left2(w128[EA_B], packed_b[p])], axis=1
            )
            right = right2(wide, w256[ER])
            shift = shift_of(4 * me + p)
            raw = operate(right, shift)
            joined = join_rows(join_cols(raw))
            from_below = edge_r[0, pl.ds(2 * p + 1, 1), :]
            from_above = edge_r[1, pl.ds(2 * p, 1), :]
            joined = (
                joined
                + jnp.where(row_ids == 0, from_below, 0.0)
                + jnp.where(row_ids == ROWS - 1, from_above, 0.0)
            )
            raw2 = operate(joined, shift)
            inner = nodes[2]
            b_s[p] = right
            v_s[p] = joined
            mrow[p] = jnp.concatenate(
                [
                    total(inner * right * right),
                    total(right * raw),
                    total(inner * joined * joined),
                    total(joined * raw2),
                    jnp.zeros((4, 128), F32),
                ],
                axis=0,
            )
            return carry

        lax.fori_loop(0, 4, mode_step, 0)

        sums = jnp.sum(
            jnp.concatenate([mrow[p] for p in range(4)], axis=0), axis=1, keepdims=True
        )
        row32, lane32 = sublanes((32, 128)), lanes((32, 128))
        mine = (row32 % 8 < 4) & (lane32 // 8 == (row32 // 8) * 4 + row32 % 8)
        moments = jnp.sum(jnp.where(mine, sums, 0.0), axis=0, keepdims=True)
        mom_s[...] = moments
        mom_r[z] = moments

        def send_moments(k, carry):
            pltpu.make_async_remote_copy(
                src_ref=mom_s,
                dst_ref=mom_r.at[z],
                send_sem=ms,
                recv_sem=mr_sem,
                device_id=(me, lax.rem(z + k, NZ)),
                device_id_type=MESH,
            ).start()
            return carry

        lax.fori_loop(1, NZ, send_moments, 0)
        view = mom_r.at[pl.ds(0, NZ - 1)]
        pltpu.make_async_copy(view, view, mr_sem).wait()
        pooled = mom_r[0]
        for at in range(1, NZ):
            pooled = pooled + mom_r[at]
        m0 = pooled
        m1, m2, m3 = (roll(pooled, -8 * k, 1) for k in range(1, 4))
        alpha0 = m0 / m1
        norm1 = alpha0 * alpha0 * m2 - m0
        gain = 1.0 + norm1 / m0
        curve = gain * gain * m1 - 2.0 * gain * alpha0 * m2 + alpha0 * alpha0 * m3
        alpha1 = norm1 / curve
        on_right = alpha0 + alpha1 * gain
        on_image = -alpha1 * alpha0
        lane1 = lanes((1, 128))
        for p in range(4):
            pick = lane1 == 32 * p
            first = jnp.sum(jnp.where(pick, on_right, 0.0), axis=1, keepdims=True)
            second = jnp.sum(jnp.where(pick, on_image, 0.0), axis=1, keepdims=True)
            out_ref[p] = first * b_s[p] + second * v_s[p]

        pltpu.make_async_copy(view, view, ms).wait()
        await_tiles(recv1.at[0], NF - 1, s1.at[0])
        await_tiles(recv2, NF - 1, s2.at[0])

        @pl.when(owner1)
        def _():
            await_tiles(recv1.at[1], UNITS - FIRST - 1, s1.at[1])
            await_tiles(recv2, NF - 1, s2.at[1])

        @pl.when(jnp.logical_not(owner1))
        def _():
            await_tiles(recv1.at[1], UNITS - FIRST, s1.at[1])

    return kernel


def solution(mesh):
    w256, w128, nodes, stiffness = tables()
    kernel = make_kernel(stiffness)

    def shards(vel_az, vel_rad, axial, metric_az, metric_rad):
        field = (4, ROWS, COLS)
        return pl.pallas_call(
            kernel,
            out_shape=jax.ShapeDtypeStruct(field, F32),
            in_specs=[pl.BlockSpec(memory_space=pltpu.HBM)] * 8,
            out_specs=pl.BlockSpec(memory_space=pltpu.VMEM),
            scratch_shapes=[
                pltpu.VMEM(field, F32),
                pltpu.VMEM(field, F32),
                pltpu.VMEM(field, F32),
                pltpu.VMEM((EZ, 32), F32),
                pltpu.VMEM((EZ, 32), F32),
                pltpu.VMEM(w256.shape, BF16),
                pltpu.VMEM(w128.shape, BF16),
                pltpu.VMEM(nodes.shape, F32),
                pltpu.VMEM((2, ROWS, COLS), F32),
                pltpu.VMEM((ROWS, COLS), F32),
                pltpu.VMEM((2, ROWS, COLS), F32),
                pltpu.VMEM((4, ROWS, 128), F32),
                pltpu.VMEM((4, ROWS, 128), F32),
                pltpu.VMEM((PADDED * 8, 128), F32),
                pltpu.VMEM((2, NF * 8, 128), F32),
                pltpu.VMEM((2, NF * 8, 128), F32),
                pltpu.VMEM((PADDED * 8, 128), F32),
                pltpu.VMEM((8, COLS), F32),
                pltpu.VMEM((2, 8, COLS), F32),
                pltpu.VMEM((8, COLS), F32),
                pltpu.VMEM((2, 8, COLS), F32),
                pltpu.VMEM(field, F32),
                pltpu.VMEM(field, F32),
                pltpu.VMEM((4, 8, 128), F32),
                pltpu.VMEM((1, 128), F32),
                pltpu.VMEM((NZ, 1, 128), F32),
                pltpu.SemaphoreType.DMA((8,)),
                pltpu.SemaphoreType.DMA((2,)),
                pltpu.SemaphoreType.DMA((2,)),
                pltpu.SemaphoreType.DMA((2,)),
                pltpu.SemaphoreType.DMA((2,)),
                pltpu.SemaphoreType.DMA((4,)),
                pltpu.SemaphoreType.DMA((4,)),
                pltpu.SemaphoreType.DMA(()),
                pltpu.SemaphoreType.DMA(()),
            ],
            compiler_params=pltpu.CompilerParams(
                collective_id=0, has_side_effects=True, vmem_limit_bytes=56 * 2**20
            ),
        )(
            vel_az,
            vel_rad,
            axial,
            metric_az,
            metric_rad,
            jnp.asarray(w256),
            jnp.asarray(w128),
            jnp.asarray(nodes),
        )

    spec = P("fourier", "elem", None)
    metric_spec = P("elem", None)
    return jax.shard_map(
        shards,
        mesh=mesh,
        in_specs=(spec, spec, spec, metric_spec, metric_spec),
        out_specs=spec,
        check_vma=False,
    )
```

time: 213 us -> 63 us (0.30)
  blocking collectives: 86.9 us -> 0 us
  Pallas kernels: 0 us -> 60.9 us
  starting transfers between devices: 50.4 us -> 0 us
  waiting for transfers between devices: 38.7 us -> 0 us
  local copies, waits for them, and re-layouts: 17.1 us -> 1.87 us
  other arithmetic: 9.73 us -> 0 us
  matrix products: 9.34 us -> 0 us
    psum x3 -> x0, blocking collectives: 86.9 us -> none  [the longest x2 57.5 us: squares(): return lax.psum(local_inner(field, field), 'elem')]
    pallas_call x0 -> x1, Pallas kernels: none -> 60.9 us  [shards(): pl.pallas_call(kernel, out_shape=jax.ShapeDtypeStruct(field, F32), in_spe...]
    all_to_all x2 -> x0, waiting for transfers between devices: 35.2 us -> none  [the longest x1 17.9 us: shards(): lax.all_to_all(drive, 'fourier', split_axis=1, concat_axis=0, tiled=True)]
    ppermute x6 -> x0, starting transfers between devices: 27.7 us -> none  [the longest x3 20 us: padded_2(): lax.ppermute(lax.slice_in_dim(block, 0, width, axis=dim), axis, backward)]
    all_to_all x2 -> x0, starting transfers between devices: 22.7 us -> none  [the longest x1 17.2 us: shards(): lax.all_to_all(drive, 'fourier', split_axis=1, concat_axis=0, tiled=True)]
    mul x10 -> x0, local copies, waits for them, and re-layouts: 11.3 us -> none  [the longest x1 4.11 us: shards(): deriv_rad = jnp.kron(eye_rad, derivative)]
    dot_general x10 -> x0, matrix products: 9.34 us -> none  [the longest x1 1.78 us: shards(): jnp.einsum('ab,pbr->par', deriv_az, axial, precision=HIGH) * metric_a]
    mul x3 -> x0, other arithmetic: 6.04 us -> none  [the longest x1 5.03 us: shards(): deriv_rad = jnp.kron(eye_rad, derivative)]
  transfers between devices with their start and end apart: 8 -> 0, of which waited for: 4 -> 0; matrix products, arithmetic and copies ran while one was open for 3% -> 0% of each run, Pallas kernels for 0% -> 0%
where the time goes in v1:
time: 63 us; the launch traced here: 62.8 us
  Pallas kernels  60.9 us (97%)
  local copies, waits for them, and re-layouts  1.87 us (3%)
    pallas_call x1, Pallas kernels, shards(): pl.pallas_call(kernel, out_shape=jax.ShapeDtypeStruct(field, F32), in_spe...  60.9 us
    unnamed x1, local copies, waits for them, and re-layouts  1.87 us

profile of v1, /device:TPU:16, one launch (start us, length us, event | category | flops | bytes accessed | tf_op | source)
XLA Modules:
  0.0 62.8 jit_solution(535822541199645978)
XLA Ops:
  0.0 60.9 %shard_map.82 = f32[4,128,256]{2,1,0:T(8,128)} custom-call(f32[4,128,256]{2,1,0:T(8,128)} %va_hbm.1, f32[4,128,256]{2,1,0:T(8,128)} %vr_hbm.1, f32[4,128,256]{2,1,0:T(8,128)} %ax_hbm.1, f32[16,32]{1,0:T(8,128)} %ma_hbm.1, f32[16,32]{1,0:T(8,128)} %mr_hbm.1, bf16[8,256,256]{2,1,0:T(8,128)(2,1)} %constant.6.clone.w256_hbm, ...), custom_call_target="tpu_custom_call" | custom-call | tf_op jit(solution)/shard_map/pallas_call | solution.py:690
  60.9 1.9 %copy.10 = f32[4,128,256]{2,1,0:T(8,128)} copy(f32[4,128,256]{2,1,0:T(8,128)} %shard_map.82) | data formatting | bytes 1048576

commit v2 on v1

v2 whole, which is shorter than its diff:
```python
import math

import jax
import jax.numpy as jnp
import ml_dtypes
import numpy as np
from jax import lax
from jax.experimental import pallas as pl
from jax.experimental.pallas import tpu as pltpu
from jax.sharding import PartitionSpec as P

MESH = pl.DeviceIdType.MESH
F32 = jnp.float32
BF16 = jnp.bfloat16
HIGH = lax.Precision.HIGHEST

PLANES = 256
NODES = 8
NF = 64
NZ = 16
ROWS = 128
COLS = 256
EZ = 16
UNIQUE = 7 * EZ
A_UNITS = 56
X_UNIT = 56
B_BASE = 57
UNITS = 99
PADDED = 105
FIRST = 64
EXTRA = (1, 27, 45)

DR_H, DR_L, SR, KR_H, KR_L, ER, C_H, C_L = range(8)
RA_B, EA_B = range(2)


def gll_tables():
    points = np.array(
        [
            -1.0,
            -0.8717401485096066,
            -0.5917001814331423,
            -0.2092992179024789,
            0.2092992179024789,
            0.5917001814331423,
            0.8717401485096066,
            1.0,
        ]
    )
    gll_weights = np.array(
        [
            0.03571428571428571,
            0.2107042271435061,
            0.3411226924835044,
            0.4124587946587038,
            0.4124587946587038,
            0.3411226924835044,
            0.2107042271435061,
            0.03571428571428571,
        ]
    )
    number = points.shape[0]
    scales = np.array(
        [
            np.prod([points[col_at] - points[other] for other in range(number) if other != col_at])
            for col_at in range(number)
        ]
    )
    derivative = np.zeros((number, number))
    for row_at in range(number):
        for col_at in range(number):
            if row_at != col_at:
                derivative[row_at, col_at] = scales[row_at] / (
                    scales[col_at] * (points[row_at] - points[col_at])
                )
    for row_at in range(number):
        derivative[row_at, row_at] = -np.sum(derivative[row_at])
    stiffness = derivative.T @ (gll_weights[:, None] * derivative)
    return (
        gll_weights.astype(np.float32),
        derivative.astype(np.float32),
        stiffness.astype(np.float32),
    )


def mode_table():
    modes = np.arange(PLANES)
    waves = np.where(modes == 1, PLANES // 2, modes // 2)
    phase = waves[:, None] * np.arange(PLANES)[None, :] % PLANES
    angles = phase * (2.0 * math.pi / PLANES)
    odd = (modes % 2 == 1) & (modes > 1)
    return (np.where(odd[:, None], -np.sin(angles), np.cos(angles)) / math.sqrt(PLANES)).astype(
        np.float32
    )


def halves(matrix):
    high = matrix.astype(ml_dtypes.bfloat16)
    low = (matrix - high.astype(np.float32)).astype(ml_dtypes.bfloat16)
    return [high, low]


def row_map():
    every = [(e, j) for e in range(EZ) for j in range(7)]
    second = {}
    for g in range(2):
        for q in range(4):
            j = g * 4 + q
            second[q * 16 + g] = (0, j) if j < 7 else (1, 0)
            if j < 7:
                second[(4 + q) * 16 + g] = (EZ - 1, j)
    left = [r for r in every if r not in second.values()]
    for block in range(8):
        for g in range(14):
            if block * 16 + g not in second:
                second[block * 16 + g] = left.pop(0)
    return second


def tables():
    weights, derivative, stiffness = gll_tables()
    w256 = halves(np.kron(np.eye(32, dtype=np.float32), derivative).T)
    fold = np.zeros((COLS, COLS), np.float32)
    for s in range(COLS):
        c = 7 * (s // 8) + s % 8
        if c < 224:
            fold[s, c] = 1.0
    w256 += [fold.astype(ml_dtypes.bfloat16)]
    w256 += halves(np.kron(np.eye(32, dtype=np.float32), stiffness).T)
    w256 += [fold.T.astype(ml_dtypes.bfloat16)]
    w256 += halves(mode_table())
    fold_rows = np.zeros((ROWS, ROWS), np.float32)
    for at, (e, j) in row_map().items():
        fold_rows[at, j * EZ + e] = 1.0
        if j == 0 and e > 0:
            fold_rows[at, 7 * EZ + e - 1] = 1.0
    unfold_rows = fold_rows.T.copy()
    unfold_rows[ROWS - 1, 14] = 1.0
    w128 = [m.astype(ml_dtypes.bfloat16) for m in (fold_rows, unfold_rows)]
    return np.stack(w256), np.stack(w128), weights, derivative, stiffness


def split(x):
    high = x.astype(BF16)
    return high, (x - high.astype(F32)).astype(BF16)


def dot(a, b):
    return jnp.dot(a, b, preferred_element_type=F32)


def left3(high, low, x):
    xh, xl = split(x)
    return dot(high, xh) + dot(high, xl) + dot(low, xh)


def right3(x, high, low):
    xh, xl = split(x)
    return dot(xh, high) + dot(xl, high) + dot(xh, low)


def right2(x, matrix):
    xh, xl = split(x)
    return dot(xh, matrix) + dot(xl, matrix)


def roll(x, shift, axis):
    size = x.shape[axis]
    shift %= size
    return pltpu.roll(x, shift, axis) if shift else x


def lanes(shape):
    return lax.broadcasted_iota(jnp.int32, shape, 1)


def sublanes(shape):
    return lax.broadcasted_iota(jnp.int32, shape, 0)


def join_cols(field):
    lane = lanes(field.shape)
    total = (
        field
        + jnp.where((lane % 8 == 7), roll(field, -1, 1), 0.0)
        + jnp.where((lane % 8 == 0) & (lane > 0), roll(field, 1, 1), 0.0)
    )
    return jnp.where(lane == COLS - 1, 0.0, total)


def along(matrix, slabs, j):
    total = float(matrix[j, 0]) * slabs[0]
    for i in range(1, NODES):
        total = total + float(matrix[j, i]) * slabs[i]
    return total


def make_kernel(weights, derivative, stiffness):
    def kernel(
        va_hbm,
        vr_hbm,
        ax_hbm,
        ma_hbm,
        mr_hbm,
        w256_hbm,
        w128_hbm,
        b_s,
        v_s,
        factors,
        va,
        vr,
        ax,
        ma_s,
        mr_s,
        w256,
        w128,
        metric,
        x_s,
        packed_b,
        send1,
        recv1,
        send2,
        recv2,
        meet_s,
        meet_r,
        edge_s,
        edge_r,
        edge_image,
        edge_right,
        mrow,
        mom_s,
        mom_r,
        in_sem,
        s1,
        r1,
        s2,
        r2,
        hs,
        hr,
        ms,
        mr_sem,
    ):
        me = lax.axis_index("fourier")
        z = lax.axis_index("elem")
        up, down = lax.rem(z + 1, NZ), lax.rem(z + NZ - 1, NZ)

        barrier = pltpu.get_barrier_semaphore()

        def far_first(k, size):
            step = (k + 1) // 2
            return size // 2 + step * (1 - 2 * lax.rem(k, 2))

        def peer_f(k):
            row, col, core = me // 8, lax.rem(me // 2, 4), lax.rem(me, 2)
            row = lax.rem(row + far_first(k // 8, 8), 8)
            col = lax.rem(col + far_first(lax.rem(k // 2, 4), 4), 4)
            core = lax.rem(core + 1 + lax.rem(k, 2), 2)
            return row * 8 + col * 2 + core

        def peer_z(k):
            return lax.rem(z + far_first(k, NZ), NZ)

        def greet_f(k, carry):
            pl.semaphore_signal(barrier, inc=1, device_id=(peer_f(k), z), device_id_type=MESH)
            return carry

        def greet_z(k, carry):
            pl.semaphore_signal(barrier, inc=1, device_id=(me, peer_z(k)), device_id_type=MESH)
            return carry

        lax.fori_loop(0, NZ - 1, greet_z, 0, unroll=True)
        lax.fori_loop(0, NF - 1, greet_f, 0, unroll=True)

        loads = [
            pltpu.make_async_copy(src, dst, in_sem.at[i])
            for i, (src, dst) in enumerate(
                [(ma_hbm, ma_s), (mr_hbm, mr_s)]
                + [(ref.at[p, :, pl.ds(128 * h, 128)], to.at[p, h]) for p in range(4) for ref, to in ((ax_hbm, ax), (va_hbm, va), (vr_hbm, vr)) for h in range(2)]
                + [(w256_hbm.at[pl.ds(0, KR_H)], w256.at[pl.ds(0, KR_H)]), (w128_hbm, w128)]
            )
        ]
        late = pltpu.make_async_copy(
            w256_hbm.at[pl.ds(KR_H, 8 - KR_H)], w256.at[pl.ds(KR_H, 8 - KR_H)], in_sem.at[28]
        )
        for load in loads:
            load.start()
        recv2[pl.ds(UNITS * 8, (PADDED - UNITS) * 8), :] = jnp.zeros(
            ((PADDED - UNITS) * 8, 128), F32
        )

        for load in loads[:2]:
            load.wait()
        up_cols = (sublanes((32, COLS)) == lanes((32, COLS)) // 8).astype(F32)
        wide = jnp.dot(
            jnp.concatenate([ma_s[...], mr_s[...]], axis=0),
            up_cols,
            precision=HIGH,
            preferred_element_type=F32,
        )
        metric_a, metric_r = wide[:EZ], wide[EZ:]

        def end_weights(shape):
            place = lanes(shape) % 8
            place = jnp.minimum(place, 7 - place)
            value = jnp.full(shape, float(weights[3]), F32)
            for at in range(3):
                value = jnp.where(place == at, float(weights[at]), value)
            return value

        weight_r = end_weights((1, COLS))
        metric[0] = metric_a
        metric[1] = metric_r
        metric[2] = weight_r / (metric_a * metric_r)
        metric[3] = metric_a / metric_r * weight_r
        metric[4] = metric_r / metric_a
        meet_s[...] = jnp.zeros((8, COLS), F32)
        for row, values in enumerate((metric_a, metric_r)):
            meet_s[2 * row : 2 * row + 1, :] = values[0:1]
            meet_s[2 * row + 1 : 2 * row + 2, :] = values[EZ - 1 :]

        for load in loads[26:]:
            load.wait()

        lane128 = lanes((16, 128))

        row16 = sublanes((EZ, COLS))
        for p in range(4):
            for load in loads[2 + 6 * p : 8 + 6 * p]:
                load.wait()

            def slab_of(ref, j, p=p):
                return jnp.concatenate(
                    [ref[p, h, pl.ds(j, EZ, stride=8), :] for h in range(2)], axis=1
                )

            slabs = [slab_of(ax, j) for j in range(NODES)]
            for j in range(NODES):
                x_s[j * EZ : (j + 1) * EZ, :] = slabs[j]
            x_all = x_s[...]
            grad_r = right3(x_all, w256[DR_H], w256[DR_L])
            loaded = []
            for j in range(NODES):
                grad_a = along(derivative, slabs, j)
                nonlinear = slab_of(va, j) * (grad_a * metric[0]) + slab_of(vr, j) * (
                    grad_r[j * EZ : (j + 1) * EZ] * metric[1]
                )
                loaded.append(
                    (2.0 * slabs[j] - nonlinear) * ((2.0 * float(weights[j])) * metric[2])
                )
            folded = right2(jnp.concatenate(loaded, axis=0), w256[SR])
            last = folded[ROWS - 1 :]
            for h in range(2):
                send1[X_UNIT * 8 + 2 * p + h : X_UNIT * 8 + 2 * p + h + 1, :] = last[
                    :, 128 * h : 128 * h + 128
                ]
            start = folded[:EZ, :128] + jnp.where(
                row16[:, :128] > 0, roll(folded[7 * EZ :, :128], 1, 0), 0.0
            )
            for j in range(7):
                slab = start if j == 0 else folded[j * EZ : (j + 1) * EZ, :128]
                for h in range(2):
                    send1[pl.ds(64 * j + 2 * p + h, 8, stride=8), :] = slab[8 * h : 8 * h + 8]
            high, low = split(folded[:, 128:])
            packed = dot(w128[RA_B], high) + dot(w128[RA_B], low)
            for h in range(2):
                quarters = [packed[(4 * h + q) * 16 : (4 * h + q + 1) * 16] for q in range(4)]
                for t in range(3):
                    tile = roll(quarters[0], -32 * t, 1)
                    for q in range(1, 4):
                        tile = jnp.where(lane128 >= 32 * q, roll(quarters[q], 32 * (q - t), 1), tile)
                    send1[pl.ds((B_BASE + t) * 8 + 2 * p + h, 16, stride=24), :] = tile
        late.start()

        pl.semaphore_wait(barrier, NF - 1 + NZ - 1)

        def exchange(src, dst, at):
            copies = [
                pltpu.make_async_remote_copy(
                    src_ref=src,
                    dst_ref=dst.at[side],
                    send_sem=hs.at[at + side],
                    recv_sem=hr.at[at + side],
                    device_id=(me, target),
                    device_id_type=MESH,
                )
                for side, target in ((0, up), (1, down))
            ]
            for copy in copies:
                copy.start()
            return copies

        def tile_at(index):
            return pl.ds(pl.multiple_of(index * 8, 8), 8)

        def send_plane(unit, slot, target):
            pltpu.make_async_remote_copy(
                src_ref=send1.at[tile_at(unit), :],
                dst_ref=recv1.at[slot, tile_at(me), :],
                send_sem=s1.at[slot],
                recv_sem=r1.at[slot],
                device_id=(target, z),
                device_id_type=MESH,
            ).start()

        def first_chunk(k, carry):
            target = peer_f(k)
            send_plane(target, 0, target)
            return carry

        def second_chunk(k, carry):
            row = lax.rem(me // 8 + far_first(k // 4, 8), 8)
            col = lax.rem(me // 2 + far_first(lax.rem(k, 4), 4), 4)
            chip = row * 4 + col

            @pl.when(2 * chip != me)
            def _():
                send_plane(FIRST + chip, 1, 2 * chip)

            return carry

        for at, target in enumerate(EXTRA):

            @pl.when(me != target)
            def _(at=at, target=target):
                send_plane(FIRST + NF // 2 + at, 1, target)

        lax.fori_loop(0, NF - 1, first_chunk, 0, unroll=True)
        meets = exchange(meet_s, meet_r, 0)
        lax.fori_loop(0, NF // 2, second_chunk, 0, unroll=True)
        unit1 = FIRST + me // 2
        owner1 = me % 2 == 0
        for at, target in enumerate(EXTRA):
            unit1 = jnp.where(me == target, FIRST + NF // 2 + at, unit1)
            owner1 = owner1 | (me == target)

        recv1[0, tile_at(me), :] = send1[tile_at(me), :]

        def await_tiles(ref, count, sem):
            view = ref.at[pl.ds(0, count * 8), :]
            pltpu.make_async_copy(view, view, sem).wait()

        def transform(slot, unit):
            x = jnp.concatenate(
                [recv1[slot, pl.ds(h, PLANES, stride=2), :] for h in range(2)], axis=1
            )
            y = left3(w256[C_H], w256[C_L], x)
            for h in range(2):
                send2[slot, pl.ds(h, PLANES, stride=2), :] = y[:, 128 * h : 128 * (h + 1)]

            def send_modes(k, carry):
                target = peer_f(k)
                pltpu.make_async_remote_copy(
                    src_ref=send2.at[slot, tile_at(target), :],
                    dst_ref=recv2.at[tile_at(unit), :],
                    send_sem=s2.at[slot],
                    recv_sem=r2.at[slot],
                    device_id=(target, z),
                    device_id_type=MESH,
                ).start()
                return carry

            lax.fori_loop(0, NF - 1, send_modes, 0, unroll=True)
            recv2[tile_at(unit), :] = send2[slot, tile_at(me), :]

        late.wait()
        await_tiles(recv1.at[0], NF - 1, r1.at[0])
        transform(0, me)

        @pl.when(owner1)
        def _():
            recv1[1, tile_at(me), :] = send1[tile_at(unit1), :]
            await_tiles(recv1.at[1], NF - 1, r1.at[1])
            transform(1, unit1)

        await_tiles(recv2, NF - 1, r2.at[0])
        even = sublanes((8, 128)) % 2 == 0
        lane = lanes((8, 128))
        sub = sublanes((8, COLS))
        low_side = sub % 2 == 0
        x_tile = recv2[X_UNIT * 8 : X_UNIT * 8 + 8, :]
        edge_rows = []
        for j in range(8):
            g, q = j // 4, j % 4
            start, end = (8 * j, 8 * j + 7) if j < 7 else (1, X_UNIT)
            part_a = jnp.where(
                even,
                recv2[8 * start : 8 * start + 8, :],
                recv2[8 * end : 8 * end + 8, :] if j < 7 else roll(x_tile, 1, 0),
            )
            pieces = [
                recv2[(B_BASE + 3 * g + t) * 8 : (B_BASE + 3 * g + t) * 8 + 8, :] for t in range(3)
            ]
            part_b = roll(pieces[0], -32 * q, 1)
            for t in range(1, 3):
                part_b = jnp.where(lane >= 32 * t, roll(pieces[t], 32 * (t - q), 1), part_b)
            if j == 7:
                part_b = jnp.where(even, part_b, x_tile)
            edge_rows.append(jnp.concatenate([part_a, part_b], axis=1))
        edge = right2(jnp.concatenate(edge_rows, axis=0), w256[ER])
        along_a = jnp.zeros((8, COLS), F32)
        for j in range(8):
            factor = jnp.where(low_side, float(stiffness[0, j]), float(stiffness[7, j]))
            along_a = along_a + factor * edge[8 * j : 8 * j + 8]
        chosen = jnp.where(low_side, edge[0:8], edge[56:64])
        along_r = right3(chosen, w256[KR_H], w256[KR_L])

        def edge_coef(at):
            return jnp.where(low_side, metric[at, 0:1, :], metric[at, EZ - 1 : EZ, :])

        def shift_of(mode):
            wave = jnp.where(mode == 1, PLANES // 2, mode // 2)
            return 4.0 + (wave.astype(F32) * 0.03125) * (wave.astype(F32) * 0.03125)

        edge_shift = shift_of(4 * me + sub // 2)
        end = float(weights[0])
        image = (
            edge_coef(3) * along_a
            + (end * edge_coef(4)) * along_r
            + edge_shift * (end * edge_coef(2)) * chosen
        )
        edge_s[0:8, :] = join_cols(image)
        edge_s[8:16, :] = chosen
        edges = exchange(edge_s, edge_r, 2)

        for copy in meets:
            copy.wait()
        next_a = jnp.where(low_side, meet_r[0, 1:2, :], meet_r[1, 0:1, :])
        next_r = jnp.where(low_side, meet_r[0, 3:4, :], meet_r[1, 2:3, :])
        corner = jnp.where(low_side, float(stiffness[7, 7]), float(stiffness[0, 0]))
        across = join_cols(
            next_a / next_r * weight_r * (corner * chosen)
            + (end * (next_r / next_a)) * along_r
            + edge_shift * (end * (weight_r / (next_a * next_r))) * chosen
        )

        for copy in edges:
            copy.wait()
        below, above = edge_r[0], edge_r[1]
        edge_image[...] = across + jnp.where(
            low_side, roll(below[0:8], -1, 0), roll(above[0:8], 1, 0)
        )
        edge_right[...] = jnp.where(low_side, roll(below[8:16], -1, 0), roll(above[8:16], 1, 0))

        @pl.when(owner1)
        def _():
            await_tiles(recv2, UNITS - FIRST - 1, r2.at[1])

        @pl.when(jnp.logical_not(owner1))
        def _():
            await_tiles(recv2, UNITS - FIRST, r2.at[1])

        for p in range(4):
            for h in range(2):
                pieces = [
                    recv2[pl.ds((B_BASE + t) * 8 + 2 * p + h, 16, stride=24), :] for t in range(3)
                ]
                for q in range(4):
                    part_b = roll(pieces[0], -32 * q, 1)
                    for t in range(1, 3):
                        part_b = jnp.where(
                            lane128 >= 32 * t, roll(pieces[t], 32 * (t - q), 1), part_b
                        )
                    if h == 0 and q == 0:
                        part_b = jnp.where(
                            sublanes((16, 128)) == 14, x_tile[2 * p + 1 : 2 * p + 2, :], part_b
                        )
                    packed_b[p, (4 * h + q) * 16 : (4 * h + q + 1) * 16, :] = part_b

        lane_r = lanes((1, COLS))
        inner_r = jnp.where(
            ((lane_r % 8 == 7) & (lane_r < COLS - 1)) | ((lane_r % 8 == 0) & (lane_r > 0)), 0.5, 1.0
        )

        def slabs_of(field):
            return [field[j * EZ : (j + 1) * EZ] for j in range(NODES)]

        def operate(field, shift):
            slabs = slabs_of(field)
            along_r = right3(field, w256[KR_H], w256[KR_L])
            heavy = shift * metric[2]
            return [
                metric[3] * along(stiffness, slabs, j)
                + float(weights[j])
                * (metric[4] * along_r[j * EZ : (j + 1) * EZ] + heavy * slabs[j])
                for j in range(NODES)
            ]

        def product(left, right, ends):
            total = ends * (left[0] * right[0] + left[7] * right[7])
            for j in range(1, 7):
                total = total + left[j] * right[j]
            return total

        def total(field):
            row = jnp.sum(field, axis=0, keepdims=True)
            return row[:, :128] + row[:, 128:]

        for p in range(4):
            left_cols = []
            for j in range(7):
                left_cols += [recv2[pl.ds(64 * j + 2 * p + h, 8, stride=8), :] for h in range(2)]
            first_slab = jnp.concatenate(left_cols[:2], axis=0)
            left_cols.append(
                jnp.where(
                    row16[:, :128] == EZ - 1, x_tile[2 * p : 2 * p + 1, :], roll(first_slab, -1, 0)
                )
            )
            high, low = split(packed_b[p])
            right_cols = dot(w128[EA_B], high) + dot(w128[EA_B], low)
            spread = right2(
                jnp.concatenate([jnp.concatenate(left_cols, axis=0), right_cols], axis=1), w256[ER]
            )
            x_s[...] = spread
            x_s[0:8, :] = spread[0:8] + jnp.where(
                sub == 0, edge_right[2 * p : 2 * p + 1, :], 0.0
            )
            x_s[ROWS - 8 :, :] = spread[ROWS - 8 :] + jnp.where(
                sub == 7, edge_right[2 * p + 1 : 2 * p + 2, :], 0.0
            )
            right = x_s[...]
            shift = shift_of(4 * me + p)
            raw = operate(right, shift)
            joined = join_cols(jnp.concatenate(raw, axis=0))
            low_slab, high_slab = joined[:EZ], joined[7 * EZ :]
            bottom = low_slab + jnp.where(
                row16 == 0, edge_image[2 * p : 2 * p + 1, :], roll(high_slab, 1, 0)
            )
            top = high_slab + jnp.where(
                row16 == EZ - 1, edge_image[2 * p + 1 : 2 * p + 2, :], roll(low_slab, -1, 0)
            )
            joined = jnp.concatenate([bottom, joined[EZ : 7 * EZ], top], axis=0)
            raw2 = operate(joined, shift)
            b_s[p] = right
            v_s[p] = joined
            right, joined = slabs_of(right), slabs_of(joined)
            mrow[p] = jnp.concatenate(
                [
                    total(product(right, right, 0.5) * inner_r),
                    total(product(right, raw, 1.0)),
                    total(product(joined, joined, 0.5) * inner_r),
                    total(product(joined, raw2, 1.0)),
                    jnp.zeros((4, 128), F32),
                ],
                axis=0,
            )

        sums = jnp.sum(
            jnp.concatenate([mrow[p] for p in range(4)], axis=0), axis=1, keepdims=True
        )
        row32, lane32 = sublanes((32, 128)), lanes((32, 128))
        mine = (row32 % 8 < 4) & (lane32 // 8 == (row32 // 8) * 4 + row32 % 8)
        moments = jnp.sum(jnp.where(mine, sums, 0.0), axis=0, keepdims=True)
        mom_s[...] = moments
        mom_r[z] = moments

        def send_moments(k, carry):
            pltpu.make_async_remote_copy(
                src_ref=mom_s,
                dst_ref=mom_r.at[z],
                send_sem=ms,
                recv_sem=mr_sem,
                device_id=(me, peer_z(k)),
                device_id_type=MESH,
            ).start()
            return carry

        lax.fori_loop(0, NZ - 1, send_moments, 0, unroll=True)
        view = mom_r.at[pl.ds(0, NZ - 1)]
        pltpu.make_async_copy(view, view, mr_sem).wait()
        pooled = mom_r[0]
        for at in range(1, NZ):
            pooled = pooled + mom_r[at]
        m0 = pooled
        m1, m2, m3 = (roll(pooled, -8 * k, 1) for k in range(1, 4))
        alpha0 = m0 / m1
        norm1 = alpha0 * alpha0 * m2 - m0
        gain = 1.0 + norm1 / m0
        curve = gain * gain * m1 - 2.0 * gain * alpha0 * m2 + alpha0 * alpha0 * m3
        alpha1 = norm1 / curve
        on_right = alpha0 + alpha1 * gain
        on_image = -alpha1 * alpha0
        lane1 = lanes((1, 128))
        for p in range(4):
            pick = lane1 == 32 * p
            first = jnp.sum(jnp.where(pick, on_right, 0.0), axis=1, keepdims=True)
            second = jnp.sum(jnp.where(pick, on_image, 0.0), axis=1, keepdims=True)
            factors[p] = jnp.concatenate(
                [first + jnp.zeros((1, 128), F32), second + jnp.zeros((1, 128), F32)]
                + [jnp.zeros((6, 128), F32)],
                axis=0,
            )

        pltpu.make_async_copy(view, view, ms).wait()
        await_tiles(recv1.at[0], NF - 1, s1.at[0])
        await_tiles(recv2, NF - 1, s2.at[0])

        @pl.when(owner1)
        def _():
            await_tiles(recv1.at[1], UNITS - FIRST - 1, s1.at[1])
            await_tiles(recv2, NF - 1, s2.at[1])

        @pl.when(jnp.logical_not(owner1))
        def _():
            await_tiles(recv1.at[1], UNITS - FIRST, s1.at[1])

    return kernel


def combine(right, image, factors, out, slots, sems):
    copies = []
    for p in range(4):
        mixed = factors[p, 0:1, 0:1] * right[p] + factors[p, 1:2, 0:1] * image[p]
        for h in range(2):
            for j in range(NODES):
                slots[p, h, pl.ds(j, EZ, stride=8), :] = mixed[
                    j * EZ : (j + 1) * EZ, 128 * h : 128 * h + 128
                ]
            copy = pltpu.make_async_copy(
                slots.at[p, h], out.at[p, :, pl.ds(128 * h, 128)], sems.at[2 * p + h]
            )
            copy.start()
            copies.append(copy)
    for copy in copies:
        copy.wait()


def solution(mesh):
    w256, w128, weights, derivative, stiffness = tables()
    kernel = make_kernel(weights, derivative, stiffness)

    def shards(vel_az, vel_rad, axial, metric_az, metric_rad):
        field = (4, ROWS, COLS)
        solved = pl.pallas_call(
            kernel,
            out_shape=(pltpu.VMEM(field, F32), pltpu.VMEM(field, F32), pltpu.VMEM((4, 8, 128), F32)),
            in_specs=[pl.BlockSpec(memory_space=pltpu.HBM)] * 7,
            out_specs=[pl.BlockSpec(memory_space=pltpu.VMEM)] * 3,
            scratch_shapes=[
                pltpu.VMEM((4, 2, ROWS, 128), F32),
                pltpu.VMEM((4, 2, ROWS, 128), F32),
                pltpu.VMEM((4, 2, ROWS, 128), F32),
                pltpu.VMEM((EZ, 32), F32),
                pltpu.VMEM((EZ, 32), F32),
                pltpu.VMEM(w256.shape, BF16),
                pltpu.VMEM(w128.shape, BF16),
                pltpu.VMEM((5, EZ, COLS), F32),
                pltpu.VMEM((ROWS, COLS), F32),
                pltpu.VMEM((4, ROWS, 128), F32),
                pltpu.VMEM((PADDED * 8, 128), F32),
                pltpu.VMEM((2, NF * 8, 128), F32),
                pltpu.VMEM((2, NF * 8, 128), F32),
                pltpu.VMEM((PADDED * 8, 128), F32),
                pltpu.VMEM((8, COLS), F32),
                pltpu.VMEM((2, 8, COLS), F32),
                pltpu.VMEM((16, COLS), F32),
                pltpu.VMEM((2, 16, COLS), F32),
                pltpu.VMEM((8, COLS), F32),
                pltpu.VMEM((8, COLS), F32),
                pltpu.VMEM((4, 8, 128), F32),
                pltpu.VMEM((1, 128), F32),
                pltpu.VMEM((NZ, 1, 128), F32),
                pltpu.SemaphoreType.DMA((29,)),
                pltpu.SemaphoreType.DMA((2,)),
                pltpu.SemaphoreType.DMA((2,)),
                pltpu.SemaphoreType.DMA((2,)),
                pltpu.SemaphoreType.DMA((2,)),
                pltpu.SemaphoreType.DMA((4,)),
                pltpu.SemaphoreType.DMA((4,)),
                pltpu.SemaphoreType.DMA(()),
                pltpu.SemaphoreType.DMA(()),
            ],
            compiler_params=pltpu.CompilerParams(
                collective_id=0, has_side_effects=True, vmem_limit_bytes=63488 * 1024
            ),
        )(
            vel_az,
            vel_rad,
            axial,
            metric_az,
            metric_rad,
            jnp.asarray(w256),
            jnp.asarray(w128),
        )
        return pl.pallas_call(
            combine,
            out_shape=jax.ShapeDtypeStruct(field, F32),
            in_specs=[pl.BlockSpec(memory_space=pltpu.VMEM)] * 3,
            out_specs=pl.BlockSpec(memory_space=pltpu.HBM),
            scratch_shapes=[pltpu.VMEM((4, 2, ROWS, 128), F32), pltpu.SemaphoreType.DMA((8,))],
            compiler_params=pltpu.CompilerParams(vmem_limit_bytes=16 * 2**20),
        )(*solved)

    spec = P("fourier", "elem", None)
    metric_spec = P("elem", None)
    return jax.shard_map(
        shards,
        mesh=mesh,
        in_specs=(spec, spec, spec, metric_spec, metric_spec),
        out_specs=spec,
        check_vma=False,
    )
```

time: 63 us -> 56.9 us (0.903)
  the two profiles are of different devices: /device:TPU:16 before, /device:TPU:1 now
where the time goes in v2:
time: 56.9 us; the launch traced here: 56.3 us
  Pallas kernels  56.3 us (99%)
    pallas_call x1, Pallas kernels, shards(): pl.pallas_call(kernel, out_shape=(pltpu.VMEM(field, F32), pltpu.VMEM(fiel...  55.4 us

profile of v2, /device:TPU:1, one launch (start us, length us, event | category | flops | bytes accessed | tf_op | source)
XLA Modules:
  0.0 56.3 jit_solution(9111882334972917034)
XLA Ops:
  0.0 55.4 %shard_map.73 = (f32[4,128,256]{2,1,0:T(8,128)S(1)}, f32[4,128,256]{2,1,0:T(8,128)S(1)}, f32[4,8,128]{2,1,0:T(8,128)S(1)}) custom-call(f32[4,128,256]{2,1,0:T(8,128)} %va_hbm.1, f32[4,128,256]{2,1,0:T(8,128)} %vr_hbm.1, f32[4,128,256]{2,1,0:T(8,128)} %ax_hbm.1, f32[16,32]{1,0:T(8,128)} %ma_hbm.1, f32[16,32]{1,0:T(8,128)} %mr_hbm.1, ...), custom_call_target="tpu_custom_call" | custom-call | tf_op jit(solution)/shard_map/pallas_call | solution.py:733
  55.4 0.9 %shard_map.74 = f32[4,128,256]{2,1,0:T(8,128)} custom-call(f32[4,128,256]{2,1,0:T(8,128)S(1)} %get-tuple-element.8.right, f32[4,128,256]{2,1,0:T(8,128)S(1)} %get-tuple-element.9.image, f32[4,8,128]{2,1,0:T(8,128)S(1)} %get-tuple-element.10.factors), custom_call_target="tpu_custom_call" | custom-call | tf_op jit(solution)/shard_map/pallas_call | solution.py:784

commit v3 on v2

--- a/solution.py
+++ b/solution.py
@@ -216,6 +216,7 @@
         w128,
         metric,
         x_s,
+        r_s,
         packed_b,
         send1,
         recv1,
@@ -239,6 +240,7 @@
         hr,
         ms,
         mr_sem,
+        known,
     ):
         me = lax.axis_index("fourier")
         z = lax.axis_index("elem")
@@ -264,11 +266,8 @@
             pl.semaphore_signal(barrier, inc=1, device_id=(peer_f(k), z), device_id_type=MESH)
             return carry
 
-        def greet_z(k, carry):
-            pl.semaphore_signal(barrier, inc=1, device_id=(me, peer_z(k)), device_id_type=MESH)
-            return carry
-
-        lax.fori_loop(0, NZ - 1, greet_z, 0, unroll=True)
+        for target in (up, down):
+            pl.semaphore_signal(barrier, inc=1, device_id=(me, target), device_id_type=MESH)
         lax.fori_loop(0, NF - 1, greet_f, 0, unroll=True)
 
         loads = [
@@ -336,7 +335,7 @@
             slabs = [slab_of(ax, j) for j in range(NODES)]
             for j in range(NODES):
                 x_s[j * EZ : (j + 1) * EZ, :] = slabs[j]
-            x_all = x_s[...]
+            x_all = x_s[0:ROWS, :]
             grad_r = right3(x_all, w256[DR_H], w256[DR_L])
             loaded = []
             for j in range(NODES):
@@ -371,7 +370,7 @@
                     send1[pl.ds((B_BASE + t) * 8 + 2 * p + h, 16, stride=24), :] = tile
         late.start()
 
-        pl.semaphore_wait(barrier, NF - 1 + NZ - 1)
+        pl.semaphore_wait(barrier, NF - 1 + 2)
 
         def exchange(src, dst, at):
             copies = [
@@ -389,6 +388,16 @@
                 copy.start()
             return copies
 
+        def spread_entry(at, reach):
+            for step in (reach, NZ - reach):
+                pl.semaphore_signal(
+                    known.at[at],
+                    inc=1,
+                    device_id=(me, lax.rem(z + step, NZ)),
+                    device_id_type=MESH,
+                )
+            pl.semaphore_wait(known.at[at], 2)
+
         def tile_at(index):
             return pl.ds(pl.multiple_of(index * 8, 8), 8)
 
@@ -427,6 +436,7 @@
         lax.fori_loop(0, NF - 1, first_chunk, 0, unroll=True)
         meets = exchange(meet_s, meet_r, 0)
         lax.fori_loop(0, NF // 2, second_chunk, 0, unroll=True)
+        spread_entry(0, 1)
         unit1 = FIRST + me // 2
         owner1 = me % 2 == 0
         for at, target in enumerate(EXTRA):
@@ -465,12 +475,15 @@
         late.wait()
         await_tiles(recv1.at[0], NF - 1, r1.at[0])
         transform(0, me)
+        spread_entry(1, 2)
 
         @pl.when(owner1)
         def _():
             recv1[1, tile_at(me), :] = send1[tile_at(unit1), :]
             await_tiles(recv1.at[1], NF - 1, r1.at[1])
             transform(1, unit1)
+
+        spread_entry(2, 4)
 
         await_tiles(recv2, NF - 1, r2.at[0])
         even = sublanes((8, 128)) % 2 == 0
@@ -574,14 +587,11 @@
         def slabs_of(field):
             return [field[j * EZ : (j + 1) * EZ] for j in range(NODES)]
 
-        def operate(field, shift):
-            slabs = slabs_of(field)
-            along_r = right3(field, w256[KR_H], w256[KR_L])
+        def operate(slabs, along_r, shift):
             heavy = shift * metric[2]
             return [
                 metric[3] * along(stiffness, slabs, j)
-                + float(weights[j])
-                * (metric[4] * along_r[j * EZ : (j + 1) * EZ] + heavy * slabs[j])
+                + float(weights[j]) * (metric[4] * along_r[j] + heavy * slabs[j])
                 for j in range(NODES)
             ]
 
@@ -607,19 +617,25 @@
             )
             high, low = split(packed_b[p])
             right_cols = dot(w128[EA_B], high) + dot(w128[EA_B], low)
-            spread = right2(
-                jnp.concatenate([jnp.concatenate(left_cols, axis=0), right_cols], axis=1), w256[ER]
-            )
-            x_s[...] = spread
-            x_s[0:8, :] = spread[0:8] + jnp.where(
+            x_s[ROWS * p : ROWS * (p + 1), :] = jnp.concatenate(
+                [jnp.concatenate(left_cols, axis=0), right_cols], axis=1
+            )
+        x_s[...] = right2(x_s[...], w256[ER])
+        for p in range(4):
+            top = ROWS * p
+            x_s[top : top + 8, :] = x_s[top : top + 8, :] + jnp.where(
                 sub == 0, edge_right[2 * p : 2 * p + 1, :], 0.0
             )
-            x_s[ROWS - 8 :, :] = spread[ROWS - 8 :] + jnp.where(
+            top = ROWS * (p + 1) - 8
+            x_s[top : top + 8, :] = x_s[top : top + 8, :] + jnp.where(
                 sub == 7, edge_right[2 * p + 1 : 2 * p + 2, :], 0.0
             )
-            right = x_s[...]
-            shift = shift_of(4 * me + p)
-            raw = operate(right, shift)
+        r_s[...] = right3(x_s[...], w256[KR_H], w256[KR_L])
+        for p in range(4):
+            at = ROWS * p
+            b_s[p] = x_s[at : at + ROWS, :]
+            right = slabs_of(b_s[p])
+            raw = operate(right, slabs_of(r_s[at : at + ROWS, :]), shift_of(4 * me + p))
             joined = join_cols(jnp.concatenate(raw, axis=0))
             low_slab, high_slab = joined[:EZ], joined[7 * EZ :]
             bottom = low_slab + jnp.where(
@@ -629,20 +645,20 @@
                 row16 == EZ - 1, edge_image[2 * p + 1 : 2 * p + 2, :], roll(low_slab, -1, 0)
             )
             joined = jnp.concatenate([bottom, joined[EZ : 7 * EZ], top], axis=0)
-            raw2 = operate(joined, shift)
-            b_s[p] = right
             v_s[p] = joined
-            right, joined = slabs_of(right), slabs_of(joined)
-            mrow[p] = jnp.concatenate(
-                [
-                    total(product(right, right, 0.5) * inner_r),
-                    total(product(right, raw, 1.0)),
-                    total(product(joined, joined, 0.5) * inner_r),
-                    total(product(joined, raw2, 1.0)),
-                    jnp.zeros((4, 128), F32),
-                ],
-                axis=0,
-            )
+            joined = slabs_of(joined)
+            mrow[p, 0:1, :] = total(product(right, right, 0.5) * inner_r)
+            mrow[p, 1:2, :] = total(product(right, raw, 1.0))
+            mrow[p, 2:3, :] = total(product(joined, joined, 0.5) * inner_r)
+            mrow[p, 4:8, :] = jnp.zeros((4, 128), F32)
+        for p in range(4):
+            x_s[ROWS * p : ROWS * (p + 1), :] = v_s[p]
+        r_s[...] = right3(x_s[...], w256[KR_H], w256[KR_L])
+        for p in range(4):
+            at = ROWS * p
+            joined = slabs_of(v_s[p])
+            raw = operate(joined, slabs_of(r_s[at : at + ROWS, :]), shift_of(4 * me + p))
+            mrow[p, 3:4, :] = total(product(joined, raw, 1.0))
 
         sums = jnp.sum(
             jnp.concatenate([mrow[p] for p in range(4)], axis=0), axis=1, keepdims=True
@@ -744,7 +760,8 @@
                 pltpu.VMEM(w256.shape, BF16),
                 pltpu.VMEM(w128.shape, BF16),
                 pltpu.VMEM((5, EZ, COLS), F32),
-                pltpu.VMEM((ROWS, COLS), F32),
+                pltpu.VMEM((4 * ROWS, COLS), F32),
+                pltpu.VMEM((4 * ROWS, COLS), F32),
                 pltpu.VMEM((4, ROWS, 128), F32),
                 pltpu.VMEM((PADDED * 8, 128), F32),
                 pltpu.VMEM((2, NF * 8, 128), F32),
@@ -768,6 +785,7 @@
                 pltpu.SemaphoreType.DMA((4,)),
                 pltpu.SemaphoreType.DMA(()),
                 pltpu.SemaphoreType.DMA(()),
+                pltpu.SemaphoreType.REGULAR((3,)),
             ],
             compiler_params=pltpu.CompilerParams(
                 collective_id=0, has_side_effects=True, vmem_limit_bytes=63488 * 1024

time: 56.9 us -> 54.1 us (0.951)
  Pallas kernels: 56.3 us -> 53.9 us
    pallas_call x1, Pallas kernels: 55.4 us -> 53 us  [shards(): pl.pallas_call(kernel, out_shape=(pltpu.VMEM(field, F32), pltpu.VMEM(fiel...]
where the time goes in v3:
time: 54.1 us; the launch traced here: 53.9 us
  Pallas kernels  53.9 us (100%)
    pallas_call x1, Pallas kernels, shards(): pl.pallas_call(kernel, out_shape=(pltpu.VMEM(field, F32), pltpu.VMEM(fiel...  53 us

profile of v3, /device:TPU:1, one launch (start us, length us, event | category | flops | bytes accessed | tf_op | source)
XLA Modules:
  0.0 53.9 jit_solution(499581899315156281)
XLA Ops:
  0.0 53.0 %shard_map.73 = (f32[4,128,256]{2,1,0:T(8,128)S(1)}, f32[4,128,256]{2,1,0:T(8,128)S(1)}, f32[4,8,128]{2,1,0:T(8,128)S(1)}) custom-call(f32[4,128,256]{2,1,0:T(8,128)} %va_hbm.1, f32[4,128,256]{2,1,0:T(8,128)} %vr_hbm.1, f32[4,128,256]{2,1,0:T(8,128)} %ax_hbm.1, f32[16,32]{1,0:T(8,128)} %ma_hbm.1, f32[16,32]{1,0:T(8,128)} %mr_hbm.1, ...), custom_call_target="tpu_custom_call" | custom-call | tf_op jit(solution)/shard_map/pallas_call | solution.py:749
  53.0 0.9 %shard_map.74 = f32[4,128,256]{2,1,0:T(8,128)} custom-call(f32[4,128,256]{2,1,0:T(8,128)S(1)} %get-tuple-element.8.right, f32[4,128,256]{2,1,0:T(8,128)S(1)} %get-tuple-element.9.image, f32[4,8,128]{2,1,0:T(8,128)S(1)} %get-tuple-element.10.factors), custom_call_target="tpu_custom_call" | custom-call | tf_op jit(solution)/shard_map/pallas_call | solution.py:802

commit v4 on v3

--- a/solution.py
+++ b/solution.py
@@ -411,15 +411,26 @@
                 device_id_type=MESH,
             ).start()
 
-        def first_chunk(k, carry):
-            target = peer_f(k)
-            send_plane(target, 0, target)
-            return carry
-
-        def second_chunk(k, carry):
+        def chip_at(k):
             row = lax.rem(me // 8 + far_first(k // 4, 8), 8)
             col = lax.rem(me // 2 + far_first(lax.rem(k, 4), 4), 4)
-            chip = row * 4 + col
+            return row * 4 + col
+
+        def first_chunk(core):
+            def step(k, carry):
+                target = 2 * chip_at(k) + core
+                send_plane(target, 0, target)
+                return carry
+
+            lax.fori_loop(0, NF // 2 - 1, step, 0, unroll=True)
+            target = me - lax.rem(me, 2) + core
+
+            @pl.when(target != me)
+            def _():
+                send_plane(target, 0, target)
+
+        def second_chunk(k, carry):
+            chip = chip_at(k)
 
             @pl.when(2 * chip != me)
             def _():
@@ -427,13 +438,14 @@
 
             return carry
 
+        first_chunk(0)
         for at, target in enumerate(EXTRA):
 
             @pl.when(me != target)
             def _(at=at, target=target):
                 send_plane(FIRST + NF // 2 + at, 1, target)
 
-        lax.fori_loop(0, NF - 1, first_chunk, 0, unroll=True)
+        first_chunk(1)
         meets = exchange(meet_s, meet_r, 0)
         lax.fori_loop(0, NF // 2, second_chunk, 0, unroll=True)
         spread_entry(0, 1)

time: 54.1 us -> 53 us (0.980)
  Pallas kernels: 53.9 us -> 52.7 us
    pallas_call x1, Pallas kernels: 53 us -> 51.8 us  [shards(): pl.pallas_call(kernel, out_shape=(pltpu.VMEM(field, F32), pltpu.VMEM(fiel...]
where the time goes in v4:
time: 53 us; the launch traced here: 52.7 us
  Pallas kernels  52.7 us (99%)
    pallas_call x1, Pallas kernels, shards(): pl.pallas_call(kernel, out_shape=(pltpu.VMEM(field, F32), pltpu.VMEM(fiel...  51.8 us

profile of v4, /device:TPU:1, one launch (start us, length us, event | category | flops | bytes accessed | tf_op | source)
XLA Modules:
  0.0 52.7 jit_solution(16985452690067395856)
XLA Ops:
  0.0 51.8 %shard_map.73 = (f32[4,128,256]{2,1,0:T(8,128)S(1)}, f32[4,128,256]{2,1,0:T(8,128)S(1)}, f32[4,8,128]{2,1,0:T(8,128)S(1)}) custom-call(f32[4,128,256]{2,1,0:T(8,128)} %va_hbm.1, f32[4,128,256]{2,1,0:T(8,128)} %vr_hbm.1, f32[4,128,256]{2,1,0:T(8,128)} %ax_hbm.1, f32[16,32]{1,0:T(8,128)} %ma_hbm.1, f32[16,32]{1,0:T(8,128)} %mr_hbm.1, ...), custom_call_target="tpu_custom_call" | custom-call | tf_op jit(solution)/shard_map/pallas_call | solution.py:761
  51.8 0.9 %shard_map.74 = f32[4,128,256]{2,1,0:T(8,128)} custom-call(f32[4,128,256]{2,1,0:T(8,128)S(1)} %get-tuple-element.8.right, f32[4,128,256]{2,1,0:T(8,128)S(1)} %get-tuple-element.9.image, f32[4,8,128]{2,1,0:T(8,128)S(1)} %get-tuple-element.10.factors), custom_call_target="tpu_custom_call" | custom-call | tf_op jit(solution)/shard_map/pallas_call | solution.py:814
